TPU v7x, 32 devices: a whole 2x2x4 slice. The times are simulated.
32 devices in a mesh: dp: 8 (over y, x, core), tensor: 4 (over z).
Axes of the slice: x: 2, y: 2, z: 4, core: 2. Of those that a mesh axis runs over, the one named last changes fastest.
Arguments:
- inputs: float32 [1024, 2048], P(('dp', 'tensor')), parts along dimension 0, may hold values from -6 to 6
- out_grad: float32 [1024, 2048], P(('dp', 'tensor')), parts along dimension 0, may hold values from -6 to 6
- pre_saved: bfloat16 [1024, 1536], P('dp', 'tensor'), parts along dimension 0, may hold values from -6 to 6
- w_in: bfloat16 [2048, 1536], P(None, 'tensor'), may hold values from -0.125 to 0.125
- w_out_t: bfloat16 [2048, 1536], P(None, 'tensor'), may hold values from -0.15625 to 0.15625
Outputs:
- input_grad: float32 [1024, 2048], P(('dp', 'tensor')), parts along dimension 0
- grad_w_in: bfloat16 [16384, 1536], P('dp', 'tensor'), parts along dimension 0
- grad_w_out_t: bfloat16 [16384, 1536], P('dp', 'tensor'), parts along dimension 0
There are 8 independent parts, one for each index of `dp`. A program takes and returns all parts, laid end to end along the dimension named above; an argument that names none is the same for every part. Nothing has to cross between parts.
All inputs are finite; a program needn't handle non-finite values.
Results may differ from a plain program's by a relative error of at most 0.02.
Values may be sent and summed in bfloat16 or wider, within the bound.
No kernel may reach another device: no remote copies, remote signals or barrier semaphores. Data moves between devices by JAX's collectives and lax.ppermute only.
A program may use at most 64 MiB of HBM per device.

v0:
```python
import jax
import jax.numpy as jnp
from jax import lax
from jax.sharding import PartitionSpec as P


def contract_rows(left, right):
    return lax.dot_general(
        left, right, (((0,), (0,)), ((), ())), preferred_element_type=jnp.float32
    )


def contract_cols(left, right):
    return lax.dot_general(
        left, right, (((1,), (1,)), ((), ())), preferred_element_type=jnp.float32
    )


def row_block(rows_grad, rows_pre, w_out_t):
    activ = jnp.maximum(rows_pre, jnp.zeros_like(rows_pre))
    back = jnp.dot(rows_grad, w_out_t, preferred_element_type=jnp.float32)
    hid_grad = jnp.where(rows_pre > 0.0, back, 0.0).astype(jnp.bfloat16)
    return (hid_grad, activ)


def on_device(inputs, out_grad, pre_saved, w_in, w_out_t):
    inputs_bf = inputs.astype(jnp.bfloat16)
    grad_bf = out_grad.astype(jnp.bfloat16)
    all_in, all_grad = (
        lax.all_gather(inputs_bf, "tensor", axis=0, tiled=True),
        lax.all_gather(grad_bf, "tensor", axis=0, tiled=True),
    )
    hid_grad, activ = row_block(all_grad, pre_saved, w_out_t)
    sum_out = contract_rows(all_grad, activ)
    sum_in = contract_rows(all_in, hid_grad)
    input_grad = lax.psum_scatter(
        contract_cols(hid_grad, w_in).astype(jnp.bfloat16),
        "tensor",
        scatter_dimension=0,
        tiled=True,
    ).astype(jnp.float32)
    return (input_grad, sum_in.astype(jnp.bfloat16), sum_out.astype(jnp.bfloat16))


def solution(mesh):
    in_specs = (
        P(("dp", "tensor"), None),
        P(("dp", "tensor"), None),
        P("dp", "tensor"),
        P(None, "tensor"),
        P(None, "tensor"),
    )
    out_specs = (P(("dp", "tensor"), None), P("dp", "tensor"), P("dp", "tensor"))
    return jax.shard_map(
        on_device, mesh=mesh, in_specs=in_specs, out_specs=out_specs, check_vma=False
    )
```

profile of v0, /device:TPU:0, one launch (start us, length us, event | category | flops | bytes accessed | tf_op | source)
XLA Modules:
  0.0 63.5 jit_solution(13251852517772152578)
XLA Ops:
  7.2 0.0 copy-start
  7.2 0.0 reduce-scatter.2.cloned.1.call-start
  7.2 1.1 %convert_element_type.27 = bf16[32,2048]{1,0:T(8,128)(2,1)S(1)} convert(f32[32,2048]{1,0:T(8,128)} %param.6) | non-fusion elementwise | flops 65536 | bytes 393216 | tf_op jit(solution)/shard_map/convert_element_type | solution.py:28
  8.3 17.4 %all_gather.6 = bf16[128,2048]{1,0:T(8,128)(2,1)S(1)} all-gather(bf16[32,2048]{1,0:T(8,128)(2,1)S(1)} %convert_element_type.27), channel_id=1, replica_groups=mesh['dp'=8,'tensor'=4] {'tensor'}, dimensions={0}, use_global_device_ids=true | all-gather | bytes 655360 | tf_op jit(solution)/shard_map/all_gather | solution.py:31
  25.7 0.0 copy-start.1
  25.7 0.8 %copy-done.1 = bf16[128,2048]{1,0:T(8,128)(2,1)} copy-done((bf16[128,2048]{1,0:T(8,128)(2,1)}, bf16[128,2048]{1,0:T(8,128)(2,1)S(1)}, u32[]{:S(2)}) %copy-start.1) | copy-done | bytes 524312
  26.5 1.9 %fusion.2 = bf16[128,384]{1,0:T(8,128)(2,1)S(1)} fusion(bf16[128,2048]{1,0:T(8,128)(2,1)S(1)} %all_gather.6, bf16[2048,384]{1,0:T(8,128)(2,1)} %param.9, bf16[128,384]{1,0:T(8,128)(2,1)} %param.7), kind=kOutput, calls=%fused_computation.6 | convolution fusion | flops 201474048 | bytes 2293760 | tf_op jit(solution)/shard_map/dot_general | solution.py:21
  28.3 0.0 copy-done
  28.4 0.0 copy-start.3
  28.4 1.4 %convolution_convert_fusion.2 = bf16[128,2048]{1,0:T(8,128)(2,1)} fusion(bf16[128,384]{1,0:T(8,128)(2,1)S(1)} %fusion.2, bf16[2048,384]{1,0:T(8,128)(2,1)S(1)} %copy-done), kind=kOutput, calls=%fused_computation.4 | convolution fusion | flops 201588736 | bytes 2195456 | tf_op jit(solution)/shard_map/dot_general | solution.py:14
  29.8 0.0 reduce-scatter.2.cloned.1.call-update
  29.8 0.0 copy-done.3
  29.8 19.8 %all_gather.7 = bf16[128,2048]{1,0:T(8,128)(2,1)S(1)} all-gather(bf16[32,2048]{1,0:T(8,128)(2,1)S(1)} %convert_element_type.31), channel_id=1, replica_groups=mesh['dp'=8,'tensor'=4] {'tensor'}, dimensions={0}, use_global_device_ids=true | all-gather | bytes 655360 | tf_op jit(solution)/shard_map/all_gather | solution.py:30
  49.7 0.6 fusion
  50.3 0.0 copy-start.2
  50.3 1.6 %copy.8 = bf16[2048,384]{1,0:T(8,128)(2,1)} copy(bf16[2048,384]{0,1:T(8,128)(2,1)S(1)} %fusion) | data formatting | bytes 3145728
  51.8 0.0 copy-done.2
  51.8 1.6 %fusion.1 = bf16[2048,384]{0,1:T(8,128)(2,1)S(1)} fusion(bf16[128,2048]{1,0:T(8,128)(2,1)} %copy-done.1, bf16[128,384]{1,0:T(8,128)(2,1)S(1)} %copy-done.2), kind=kOutput, calls=%fused_computation.3 | convolution fusion | flops 202162176 | bytes 2195456 | tf_op jit(solution)/shard_map/dot_general | solution.py:8
  53.5 1.6 %copy.9 = bf16[2048,384]{1,0:T(8,128)(2,1)} copy(bf16[2048,384]{0,1:T(8,128)(2,1)S(1)} %fusion.1) | data formatting | bytes 3145728
  55.1 0.0 reduce-scatter.2.cloned.1.call-done
  55.1 1.6 %convert_element_type.30 = f32[32,2048]{1,0:T(8,128)} convert(bf16[32,2048]{1,0:T(8,128)(2,1)} %reduce-scatter.2.cloned.1.call-done) | non-fusion elementwise | flops 65536 | bytes 393216 | tf_op jit(solution)/shard_map/convert_element_type | solution.py:41
  (1 shorter events, 0.0 us)
Async XLA Ops:
  7.2 21.2 %copy-start = (bf16[2048,384]{1,0:T(8,128)(2,1)S(1)}, bf16[2048,384]{1,0:T(8,128)(2,1)}, u32[]{:S(2)}) copy-start(bf16[2048,384]{1,0:T(8,128)(2,1)} %param.8) | copy-start | bytes 4718596
  7.2 47.9 %reduce-scatter.2.cloned.1.call-start = ((), (), s32[]{:S(2)}) async-start(), calls=%async_computation.1 | async-start | bytes 655360 | tf_op jit(solution)/shard_map/reduce_scatter | solution.py:36
  25.7 0.8 %copy-start.1 = (bf16[128,2048]{1,0:T(8,128)(2,1)}, bf16[128,2048]{1,0:T(8,128)(2,1)S(1)}, u32[]{:S(2)}) copy-start(bf16[128,2048]{1,0:T(8,128)(2,1)S(1)} %all_gather.6) | copy-start | bytes 1572868
  28.4 1.5 %copy-start.3 = (f32[32,2048]{1,0:T(8,128)S(1)}, f32[32,2048]{1,0:T(8,128)}, u32[]{:S(2)}) copy-start(f32[32,2048]{1,0:T(8,128)} %param.5) | copy-start | bytes 786436
  50.3 1.6 %copy-start.2 = (bf16[128,384]{1,0:T(8,128)(2,1)S(1)}, bf16[128,384]{1,0:T(8,128)(2,1)}, u32[]{:S(2)}) copy-start(bf16[128,384]{1,0:T(8,128)(2,1)} %param.7) | copy-start | bytes 294916
Sparse Core Ops, SparseCore 0:
  29.9 24.5 reduce-scatter.1
where the time goes:
time: 63.8 us; the launch traced here: 63.5 us
  blocking collectives  37.2 us (58%)
  between operations  14.1 us (22%)
  matrix products  5.53 us (9%)
  local copies, waits for them, and re-layouts  3.96 us (6%)
  other arithmetic  2.72 us (4%)
    all_gather x1, blocking collectives, on_device(): lax.all_gather(inputs_bf, 'tensor', axis=0, tiled=True)  19.8 us
    all_gather x1, blocking collectives, on_device(): lax.all_gather(grad_bf, 'tensor', axis=0, tiled=True)  17.4 us
    unnamed x10, local copies, waits for them, and re-layouts  3.96 us
    dot_general x2, matrix products, contract_rows(): lax.dot_general(left, right, (((0,), (0,)), ((), ())), preferred_element_...  2.23 us
    dot_general x1, matrix products, row_block(): back = jnp.dot(rows_grad, w_out_t, preferred_element_type=jnp.float32)  1.88 us
    convert_element_type x1, other arithmetic, on_device(): input_grad = lax.psum_scatter(contract_cols(hid_grad, w_in).astype(jnp.bf...  1.62 us
    dot_general x1, matrix products, contract_cols(): lax.dot_general(left, right, (((1,), (1,)), ((), ())), preferred_element_...  1.42 us
  transfers between devices with their start and end apart: 1, of which 0 were waited for; matrix products, arithmetic and copies ran while one was open for 8% of the time, Pallas kernels for 0%

commit v1 on v0

v1 whole, which is shorter than its diff:
```python
import functools

import jax
import jax.numpy as jnp
from jax import lax
from jax.experimental import pallas as pl
from jax.experimental.pallas import tpu as pltpu
from jax.sharding import PartitionSpec as P

AXIS = "tensor"
HBM = pl.BlockSpec(memory_space=pl.ANY)
VMEM = pl.BlockSpec(memory_space=pltpu.VMEM)
SMEM = pl.BlockSpec(memory_space=pltpu.SMEM)
PARAMS = pltpu.CompilerParams(vmem_limit_bytes=32 * 1024 * 1024)


def largest_tile(extent, limit):
    tile = min(extent, limit)
    while extent % tile:
        tile //= 2
    return tile


def cost(flops, moved):
    return pl.CostEstimate(flops=flops, bytes_accessed=moved, transcendentals=0)


def team_of(n):
    return 2 if n % 2 == 0 else 1


def owner(me, slot, n):
    team = team_of(n)
    ahead = lax.rem(me + slot // team * team, n)
    if slot % team == 0:
        return ahead
    return ahead + 1 - 2 * lax.rem(ahead, 2)


def pre_block(ref, me, slot, n, rows):
    return ref[pl.ds(pl.multiple_of(owner(me, slot, n) * rows, rows), rows), :]


def stack(refs, starts, rows, columns=slice(None)):
    return jnp.concatenate([ref[s : s + rows, columns] for ref, s in zip(refs, starts)], axis=0)


def pair_kernel(upper_ref, lower_ref, both_ref):
    rows = upper_ref.shape[0]
    both_ref[:rows, :] = upper_ref[...]
    both_ref[rows:, :] = lower_ref[...].astype(both_ref.dtype)


def pair(upper, lower):
    rows, width = upper.shape
    return pl.pallas_call(
        pair_kernel,
        out_shape=jax.ShapeDtypeStruct((2 * rows, width), upper.dtype),
        in_specs=[VMEM] * 2,
        out_specs=VMEM,
        cost_estimate=cost(0, 10 * rows * width),
        compiler_params=PARAMS,
        name="pair",
    )(upper, lower)


def share(pre, grads, w_out_ref, w_in_ref, emit):
    back = jnp.dot(grads, w_out_ref[...], preferred_element_type=jnp.float32)
    hid = jnp.where(pre.astype(jnp.float32) > 0.0, back, 0.0).astype(jnp.bfloat16)
    width = w_in_ref.shape[0]
    tile = largest_tile(width, 512)
    for start in range(0, width, tile):
        columns = slice(start, start + tile)
        part = lax.dot_general(
            hid,
            w_in_ref[columns, :],
            (((1,), (1,)), ((), ())),
            preferred_element_type=jnp.float32,
        )
        emit(columns, part)
    return hid


def own_kernel(n, me_ref, pre_ref, w_out_ref, w_in_ref, grad_ref, hid_ref, part_ref):
    rows = part_ref.shape[0]

    def emit(columns, part):
        part_ref[:, columns] = part

    pre = pre_block(pre_ref, me_ref[0], 0, n, rows)
    hid_ref[...] = share(pre, grad_ref[...], w_out_ref, w_in_ref, emit)


def own_block(n, me, pre, w_out_t, w_in, grad):
    hidden, width = pre.shape[1], w_in.shape[0]
    rows = pre.shape[0] // n
    return pl.pallas_call(
        functools.partial(own_kernel, n),
        out_shape=[
            jax.ShapeDtypeStruct((rows, hidden), jnp.bfloat16),
            jax.ShapeDtypeStruct((rows, width), jnp.float32),
        ],
        in_specs=[SMEM] + [VMEM] * 4,
        out_specs=[VMEM] * 2,
        cost_estimate=cost(4 * rows * width * hidden, 4 * width * hidden + 6 * rows * width),
        compiler_params=PARAMS,
        name="own_block",
    )(me, pre, w_out_t, w_in, grad)


def partial_kernel(n, starts, me_ref, pre_ref, w_out_ref, w_in_ref, *refs):
    grad_refs, hid_ref, part_refs = refs[: n - 1], refs[n - 1], refs[n:]
    rows = part_refs[0].shape[0]
    me = me_ref[0]

    def emit(columns, part):
        part = part.astype(jnp.bfloat16)
        for k, ref in enumerate(part_refs):
            ref[:, columns] = part[k * rows : (k + 1) * rows]

    pre = jnp.concatenate([pre_block(pre_ref, me, k, n, rows) for k in range(1, n)], axis=0)
    hid_ref[...] = share(pre, stack(grad_refs, starts, rows), w_out_ref, w_in_ref, emit)


def partials(n, me, pre, w_out_t, w_in, pieces):
    hidden, width = pre.shape[1], w_in.shape[0]
    count = n - 1
    rows = pre.shape[0] // n
    grads, starts = zip(*pieces)
    return pl.pallas_call(
        functools.partial(partial_kernel, n, starts),
        out_shape=[jax.ShapeDtypeStruct((count * rows, hidden), jnp.bfloat16)]
        + [jax.ShapeDtypeStruct((rows, width), jnp.bfloat16)] * count,
        in_specs=[SMEM] + [VMEM] * (count + 3),
        out_specs=[VMEM] * (count + 1),
        cost_estimate=cost(
            4 * count * rows * width * hidden,
            4 * count * rows * (width + hidden) + 4 * width * hidden,
        ),
        compiler_params=PARAMS,
        name="partials",
    )(me, pre, w_out_t, w_in, *grads)


def weight_tiles(lefts, starts, right, out_hbm, buffer, sems):
    rows = right.shape[0] // len(lefts)
    moves = []
    for k in range(sems.shape[0]):
        tile = buffer.shape[0] // sems.shape[0]
        columns = slice(k * tile, (k + 1) * tile)
        buffer[columns, :] = lax.dot_general(
            stack(lefts, starts, rows, columns),
            right,
            (((0,), (0,)), ((), ())),
            preferred_element_type=jnp.float32,
        ).astype(buffer.dtype)
        moves.append(pltpu.make_async_copy(buffer.at[columns], out_hbm.at[columns], sems.at[k]))
        moves[k].start()
    return moves


def out_kernel(n, starts, me_ref, pre_ref, *refs):
    left_refs, (out_hbm, buffer, sems) = refs[:n], refs[n:]
    me, rows = me_ref[0], pre_ref.shape[0] // n
    pre = jnp.concatenate([pre_block(pre_ref, me, k, n, rows) for k in range(n)], axis=0)
    activ = jnp.maximum(pre, jnp.zeros_like(pre))
    for move in weight_tiles(left_refs, starts, activ, out_hbm, buffer, sems):
        move.wait()


def in_kernel(n, starts, hid_count, *refs):
    left_refs, hid_refs, (out_hbm, buffer, sems) = refs[:n], refs[n : n + hid_count], refs[n + hid_count :]
    hid = jnp.concatenate([ref[...] for ref in hid_refs], axis=0)
    for move in weight_tiles(left_refs, starts, hid, out_hbm, buffer, sems):
        move.wait()


def weight_scratch(width, hidden):
    return [
        pltpu.VMEM((width, hidden), jnp.bfloat16),
        pltpu.SemaphoreType.DMA((width // largest_tile(width, 256),)),
    ]


def weight_cost(total, width, hidden):
    return cost(2 * total * width * hidden, 2 * total * (width + hidden) + 2 * width * hidden)


def out_weight_grad(n, me, pieces, pre):
    lefts, starts = zip(*pieces)
    width, hidden = lefts[0].shape[1], pre.shape[1]
    return pl.pallas_call(
        functools.partial(out_kernel, n, starts),
        out_shape=jax.ShapeDtypeStruct((width, hidden), jnp.bfloat16),
        in_specs=[SMEM] + [VMEM] * (n + 1),
        out_specs=HBM,
        scratch_shapes=weight_scratch(width, hidden),
        cost_estimate=weight_cost(pre.shape[0], width, hidden),
        compiler_params=PARAMS,
        name="out_weight_grad",
    )(me, pre, *lefts)


def in_weight_grad(n, pieces, hids):
    lefts, starts = zip(*pieces)
    width, hidden = lefts[0].shape[1], hids[0].shape[1]
    return pl.pallas_call(
        functools.partial(in_kernel, n, starts, len(hids)),
        out_shape=jax.ShapeDtypeStruct((width, hidden), jnp.bfloat16),
        in_specs=[VMEM] * (n + len(hids)),
        out_specs=HBM,
        scratch_shapes=weight_scratch(width, hidden),
        cost_estimate=weight_cost(sum(hid.shape[0] for hid in hids), width, hidden),
        compiler_params=PARAMS,
        name="in_weight_grad",
    )(*lefts, *hids)


def owner_of(me, slot, n):
    ahead = (me + slot // team_of(n) * team_of(n)) % n
    return ahead ^ (slot % team_of(n))


def from_slot(n, block, slot):
    return lax.ppermute(block, AXIS, [(owner_of(i, slot, n), i) for i in range(n)])


def to_slot(n, block, slot):
    return lax.ppermute(block, AXIS, [(i, owner_of(i, slot, n)) for i in range(n)])


def later(values, *things):
    return lax.optimization_barrier((values, things))[0]


def on_device(inputs, out_grad, pre_saved, w_in, w_out_t, *, n):
    team = team_of(n)
    far = range(team, n, team)
    rows = inputs.shape[0]
    me = lax.axis_index(AXIS).astype(jnp.int32).reshape(1)
    grad_bf = out_grad.astype(jnp.bfloat16)
    far_grads = [from_slot(n, grad_bf, k) for k in far]
    both = pair(grad_bf, inputs)
    grads, ins = {0: (grad_bf, 0)}, {}
    if team == 2:
        near = from_slot(n, both, 1)
        grads[1], ins[1] = (near, 0), (near, rows)
    own_hid, input_grad = own_block(n, me, pre_saved, w_out_t, w_in, grad_bf)
    hids = [own_hid]
    far_grads = later(far_grads, own_hid)
    for k, got in zip(far, far_grads):
        grads[k] = (got, 0)
        if team == 2:
            grads[k + 1] = (from_slot(n, got, 1), 0)
    inputs_bf = later(inputs, far_grads).astype(jnp.bfloat16)
    ins[0] = (inputs_bf, 0)
    far_ins = [from_slot(n, inputs_bf, k) for k in far]
    arrived, pre = [], pre_saved
    if n > 1:
        hid, *parts = partials(n, me, pre_saved, w_out_t, w_in, [grads[k] for k in range(1, n)])
        pre = later(pre, parts)
        parts = [None] + parts
        hids.append(hid)
        sums = [parts[k] + from_slot(n, parts[k + 1], 1) if team == 2 else parts[k] for k in far]
        sums, parts = lax.optimization_barrier((sums, parts))
        arrived = [to_slot(n, block, k) for k, block in zip(far, sums)]
        if team == 2:
            arrived.append(from_slot(n, parts[1], 1))
    grad_w_out_t = out_weight_grad(n, me, [grads[k] for k in range(n)], pre)
    far_ins = later(far_ins, grad_w_out_t)
    for k, got in zip(far, far_ins):
        ins[k] = (got, 0)
        if team == 2:
            ins[k + 1] = (from_slot(n, got, 1), 0)
    grad_w_in = in_weight_grad(n, [ins[k] for k in range(n)], hids)
    for block in arrived:
        input_grad = input_grad + block.astype(jnp.float32)
    return (input_grad, grad_w_in, grad_w_out_t)


def solution(mesh):
    in_specs = (
        P(("dp", AXIS), None),
        P(("dp", AXIS), None),
        P("dp", AXIS),
        P(None, AXIS),
        P(None, AXIS),
    )
    out_specs = (P(("dp", AXIS), None), P("dp", AXIS), P("dp", AXIS))
    return jax.shard_map(
        functools.partial(on_device, n=mesh.shape[AXIS]),
        mesh=mesh,
        in_specs=in_specs,
        out_specs=out_specs,
        check_vma=False,
    )
```

time: 63.8 us -> 36.8 us (0.58)
  blocking collectives: 37.2 us -> 0 us
  starting transfers between devices: 0.04 us -> 14 us
  between operations: 14.1 us -> 0.69 us
  waiting for transfers between devices: 0.02 us -> 10.6 us
  matrix products: 5.53 us -> 0 us
  Pallas kernels: 0 us -> 4.83 us
  other arithmetic: 2.72 us -> 1.75 us
  local copies, waits for them, and re-layouts: 3.96 us -> 4.67 us
    all_gather x2 -> x0, blocking collectives: 37.2 us -> none  [the longest x1 19.8 us: on_device(): lax.all_gather(inputs_bf, 'tensor', axis=0, tiled=True)]
    ppermute x0 -> x8, starting transfers between devices: none -> 14 us  [the longest x7 13.7 us: from_slot(): lax.ppermute(block, AXIS, [(owner_of(i, slot, n), i) for i in range(n)])]
    ppermute x0 -> x8, waiting for transfers between devices: none -> 10.6 us  [the longest x7 8.36 us: from_slot(): lax.ppermute(block, AXIS, [(owner_of(i, slot, n), i) for i in range(n)])]
    dot_general x4 -> x0, matrix products: 5.53 us -> none  [the longest x2 2.23 us: contract_rows(): lax.dot_general(left, right, (((0,), (0,)), ((), ())), preferred_element_...]
    pallas_call x0 -> x5, Pallas kernels: none -> 4.83 us  [the longest x1 1.47 us: out_weight_grad(): pl.pallas_call(functools.partial(out_kernel, n, starts), out_shape=jax.Sh...]
    convert_element_type x2 -> x1, other arithmetic: 1.64 us -> 0.02 us  [on_device(): inputs_bf = later(inputs, far_grads).astype(jnp.bfloat16)]
    add x0 -> x2, other arithmetic: none -> 0.77 us  [the longest x1 0.74 us: on_device(): input_grad = input_grad + block.astype(jnp.float32)]
    unnamed x10 -> x14, local copies, waits for them, and re-layouts: 3.96 us -> 4.67 us
  transfers between devices with their start and end apart: 1 -> 8, of which waited for: 0 -> 6; matrix products, arithmetic and copies ran while one was open for 8% -> 0% of each run, Pallas kernels for 0% -> 13%
where the time goes in v1:
time: 36.8 us; the launch traced here: 36.5 us
  starting transfers between devices  14 us (38%)
  waiting for transfers between devices  10.6 us (29%)
  Pallas kernels  4.83 us (13%)
  local copies, waits for them, and re-layouts  4.67 us (13%)
  other arithmetic  1.75 us (5%)
  between operations  0.69 us (2%)
    ppermute x7, starting transfers between devices, from_slot(): lax.ppermute(block, AXIS, [(owner_of(i, slot, n), i) for i in range(n)])  13.7 us
    ppermute x7, waiting for transfers between devices, from_slot(): lax.ppermute(block, AXIS, [(owner_of(i, slot, n), i) for i in range(n)])  8.36 us
    unnamed x14, local copies, waits for them, and re-layouts  4.67 us
    ppermute x1, waiting for transfers between devices, to_slot(): lax.ppermute(block, AXIS, [(i, owner_of(i, slot, n)) for i in range(n)])  2.21 us
    pallas_call x1, Pallas kernels, out_weight_grad(): pl.pallas_call(functools.partial(out_kernel, n, starts), out_shape=jax.Sh...  1.47 us
    pallas_call x1, Pallas kernels, in_weight_grad(): pl.pallas_call(functools.partial(in_kernel, n, starts, len(hids)), out_sh...  1.46 us
    convert_element_type x1, other arithmetic, on_device(): grad_bf = out_grad.astype(jnp.bfloat16)  0.97 us
    pallas_call x1, Pallas kernels, partials(): pl.pallas_call(functools.partial(partial_kernel, n, starts), out_shape=[j...  0.96 us
  transfers between devices with their start and end apart: 8, of which 6 were waited for; matrix products, arithmetic and copies ran while one was open for 0% of the time, Pallas kernels for 13%

profile of v1, /device:TPU:0, one launch (start us, length us, event | category | flops | bytes accessed | tf_op | source)
XLA Modules:
  0.0 36.5 jit_solution(9278529241553786725)
XLA Ops:
  0.6 1.0 %convert_element_type.12.grad_ref.upper_ref.refs_0_ = bf16[32,2048]{1,0:T(8,128)(2,1)S(1)} convert(f32[32,2048]{1,0:T(8,128)} %param.6) | non-fusion elementwise | flops 65536 | bytes 393216 | tf_op jit(solution)/shard_map/convert_element_type | solution.py:241
  1.6 4.1 %collective-permute-start.1 = (bf16[32,2048]{1,0:T(8,128)(2,1)S(1)}, bf16[32,2048]{1,0:T(8,128)(2,1)S(1)}, u32[]{:S(2)}, u32[]{:S(2)}) collective-permute-start(bf16[32,2048]{1,0:T(8,128)(2,1)S(1)} %convert_element_type.12.grad_ref.upper_ref.refs_0_), channel_id=1, source_target_pairs={{2,0},{3,1},{0,2},{1,3},{6,4},{7,5},{4,6},{5,7},{10,8},{11,9},{8,1... | collective-permute-start | bytes 393224 | tf_op jit(solution)/shard_map/ppermute | solution.py:225
  5.7 0.0 copy-start.4
  5.7 0.9 %copy-done.4 = f32[32,2048]{1,0:T(8,128)S(1)} copy-done((f32[32,2048]{1,0:T(8,128)S(1)}, f32[32,2048]{1,0:T(8,128)}, u32[]{:S(2)}) %copy-start.4) | copy-done | bytes 262168
  6.7 0.0 copy-start.5
  6.7 1.6 %collective-permute-start = (bf16[64,2048]{1,0:T(8,128)(2,1)S(1)}, bf16[64,2048]{1,0:T(8,128)(2,1)S(1)}, u32[]{:S(2)}, u32[]{:S(2)}) collective-permute-start(bf16[64,2048]{1,0:T(8,128)(2,1)S(1)} %pair.1), channel_id=1, source_target_pairs={{1,0},{0,1},{3,2},{2,3},{5,4},{4,5},{7,6},{6,7},{9,8},{8,9},{11,10... | collective-permute-start | bytes 786440 | tf_op jit(solution)/shard_map/ppermute | solution.py:225
  8.3 0.0 copy-start
  8.3 1.4 %copy-done = bf16[2048,384]{1,0:T(8,128)(2,1)S(1)} copy-done((bf16[2048,384]{1,0:T(8,128)(2,1)S(1)}, bf16[2048,384]{1,0:T(8,128)(2,1)}, u32[]{:S(2)}) %copy-start) | copy-done | bytes 1572888
  9.7 0.0 copy-start.2
  9.7 1.4 %copy-done.2 = bf16[2048,384]{1,0:T(8,128)(2,1)S(1)} copy-done((bf16[2048,384]{1,0:T(8,128)(2,1)S(1)}, bf16[2048,384]{1,0:T(8,128)(2,1)}, u32[]{:S(2)}) %copy-start.2) | copy-done | bytes 1572888
  11.1 0.0 copy-start.6
  11.1 0.9 %copy-done.6 = bf16[128,384]{1,0:T(8,128)(2,1)S(1)} copy-done((bf16[128,384]{1,0:T(8,128)(2,1)S(1)}, bf16[128,384]{1,0:T(8,128)(2,1)}, u32[]{:S(2)}) %copy-start.6) | copy-done | bytes 98328
  12.0 0.0 copy-start.1
  12.0 0.0 copy-start.3
  12.0 0.9 %own_block.1 = (bf16[32,384]{1,0:T(8,128)(2,1)S(1)}, f32[32,2048]{1,0:T(8,128)S(1)}) custom-call(s32[1]{0:T(128)} %bitcast.me_ref, bf16[128,384]{1,0:T(8,128)(2,1)S(1)} %copy-done.6, bf16[2048,384]{1,0:T(8,128)(2,1)S(1)} %copy-done, bf16[2048,384]{1,0:T(8,128)(2,1)S(1)} %copy-done.2, bf16[32,2048]{1,0:T(8,128)(2,1)S(1)} %convert_element_type.12.grad_ref.upper_ref.refs_0_), custom_call_target="tpu_custom_call" | custom-call | flops 100663296 | bytes 3538944 | tf_op jit(solution)/shard_map/own_block/pallas_call | solution.py:97
  13.0 0.0 collective-permute-done.1.refs_1_.refs_2_
  13.0 0.5 %collective-permute-start.2 = (bf16[32,2048]{1,0:T(8,128)(2,1)S(1)}, bf16[32,2048]{1,0:T(8,128)(2,1)S(1)}, u32[]{:S(2)}, u32[]{:S(2)}) collective-permute-start(bf16[32,2048]{1,0:T(8,128)(2,1)S(1)} %collective-permute-done.1.refs_1_.refs_2_), channel_id=1, source_target_pairs={{1,0},{0,1},{3,2},{2,3},{5,4},{4,5},{7,6},{6,7},{9,8},{8,9},{11,10... | collective-permute-start | bytes 393224 | tf_op jit(solution)/shard_map/ppermute | solution.py:225
  13.5 0.0 copy-done.5
  13.5 2.8 %collective-permute-start.6 = (bf16[32,2048]{1,0:T(8,128)(2,1)S(1)}, bf16[32,2048]{1,0:T(8,128)(2,1)S(1)}, u32[]{:S(2)}, u32[]{:S(2)}) collective-permute-start(bf16[32,2048]{1,0:T(8,128)(2,1)S(1)} %convert_element_type.15.refs_0_), channel_id=1, source_target_pairs={{2,0},{3,1},{0,2},{1,3},{6,4},{7,5},{4,6},{5,7},{10,8},{11,9},{8,1... | collective-permute-start | bytes 393224 | tf_op jit(solution)/shard_map/ppermute | solution.py:225
  16.3 2.8 %collective-permute-done.refs_0_.refs_1_ = bf16[64,2048]{1,0:T(8,128)(2,1)S(1)} collective-permute-done((bf16[64,2048]{1,0:T(8,128)(2,1)S(1)}, bf16[64,2048]{1,0:T(8,128)(2,1)S(1)}, u32[]{:S(2)}, u32[]{:S(2)}) %collective-permute-start) | collective-permute-done | bytes 262176 | tf_op jit(solution)/shard_map/ppermute | solution.py:225
  19.1 2.4 %collective-permute-done.2.refs_2_.refs_3_ = bf16[32,2048]{1,0:T(8,128)(2,1)S(1)} collective-permute-done((bf16[32,2048]{1,0:T(8,128)(2,1)S(1)}, bf16[32,2048]{1,0:T(8,128)(2,1)S(1)}, u32[]{:S(2)}, u32[]{:S(2)}) %collective-permute-start.2) | collective-permute-done | bytes 131104 | tf_op jit(solution)/shard_map/ppermute | solution.py:225
  21.5 0.0 copy-done.1
  21.5 0.0 copy-done.3
  21.5 1.0 %partials.1 = (bf16[96,384]{1,0:T(8,128)(2,1)S(1)}, bf16[32,2048]{1,0:T(8,128)(2,1)S(1)}, bf16[32,2048]{1,0:T(8,128)(2,1)S(1)}, bf16[32,2048]{1,0:T(8,128)(2,1)S(1)}) custom-call(s32[1]{0:T(128)} %bitcast.me_ref, bf16[128,384]{1,0:T(8,128)(2,1)S(1)} %copy-done.6, bf16[2048,384]{1,0:T(8,128)(2,1)S(1)} %copy-done.1, bf16[2048,384]{1,0:T(8,128)(2,1)S(1)} %copy-done.3, ...), custom_call_target="tpu_custom_call" | custom-call | flops 301989888 | bytes 4079616 | tf_op jit(solution)/shard_map/partials/pallas_call | solution.py:130
  22.4 0.1 collective-permute-start.3
  22.5 1.5 %out_weight_grad.1 = bf16[2048,384]{1,0:T(8,128)(2,1)} custom-call(s32[1]{0:T(128)} %bitcast.me_ref, bf16[128,384]{1,0:T(8,128)(2,1)S(1)} %copy-done.6, bf16[32,2048]{1,0:T(8,128)(2,1)S(1)} %convert_element_type.12.grad_ref.upper_ref.refs_0_, bf16[64,2048]{1,0:T(8,128)(2,1)S(1)} %collective-permute-done.refs_0_.refs_1_, ...), custom_call_target="tpu_custom_call" | custom-call | flops 201326592 | bytes 2195456 | tf_op jit(solution)/shard_map/out_weight_grad/pallas_call | solution.py:192
  24.0 0.0 collective-permute-done.6.refs_2_
  24.0 2.1 %collective-permute-start.7 = (bf16[32,2048]{1,0:T(8,128)(2,1)S(1)}, bf16[32,2048]{1,0:T(8,128)(2,1)S(1)}, u32[]{:S(2)}, u32[]{:S(2)}) collective-permute-start(bf16[32,2048]{1,0:T(8,128)(2,1)S(1)} %collective-permute-done.6.refs_2_), channel_id=1, source_target_pairs={{1,0},{0,1},{3,2},{2,3},{5,4},{4,5},{7,6},{6,7},{9,8},{8,9},{11,10... | collective-permute-start | bytes 393224 | tf_op jit(solution)/shard_map/ppermute | solution.py:225
  26.1 2.5 %collective-permute-done.3 = bf16[32,2048]{1,0:T(8,128)(2,1)S(1)} collective-permute-done((bf16[32,2048]{1,0:T(8,128)(2,1)S(1)}, bf16[32,2048]{1,0:T(8,128)(2,1)S(1)}, u32[]{:S(2)}, u32[]{:S(2)}) %collective-permute-start.3) | collective-permute-done | bytes 131104 | tf_op jit(solution)/shard_map/ppermute | solution.py:225
  28.6 0.3 collective-permute-start.4
  29.0 2.5 %collective-permute-start.5 = (bf16[32,2048]{1,0:T(8,128)(2,1)S(1)}, bf16[32,2048]{1,0:T(8,128)(2,1)S(1)}, u32[]{:S(2)}, u32[]{:S(2)}) collective-permute-start(bf16[32,2048]{1,0:T(8,128)(2,1)S(1)} %get-tuple-element.22), channel_id=1, source_target_pairs={{1,0},{0,1},{3,2},{2,3},{5,4},{4,5},{7,6},{6,7},{9,8},{8,9},{11,10... | collective-permute-start | bytes 393224 | tf_op jit(solution)/shard_map/ppermute | solution.py:225
  31.4 0.6 %collective-permute-done.7.refs_3_ = bf16[32,2048]{1,0:T(8,128)(2,1)S(1)} collective-permute-done((bf16[32,2048]{1,0:T(8,128)(2,1)S(1)}, bf16[32,2048]{1,0:T(8,128)(2,1)S(1)}, u32[]{:S(2)}, u32[]{:S(2)}) %collective-permute-start.7) | collective-permute-done | bytes 131104 | tf_op jit(solution)/shard_map/ppermute | solution.py:225
  32.0 1.5 %in_weight_grad.1 = bf16[2048,384]{1,0:T(8,128)(2,1)} custom-call(bf16[32,2048]{1,0:T(8,128)(2,1)S(1)} %convert_element_type.15.refs_0_, bf16[64,2048]{1,0:T(8,128)(2,1)S(1)} %collective-permute-done.refs_0_.refs_1_, bf16[32,2048]{1,0:T(8,128)(2,1)S(1)} %collective-permute-done.6.refs_2_, bf16[32,2048]{1,0:T(8,128)(2,1)S(1)} %collective-permute-done.7.refs_3_, ...), custom_call_target="tpu_custom_call" | custom-call | flops 201326592 | bytes 2195456 | tf_op jit(solution)/shard_map/in_weight_grad/pallas_call | solution.py:207
  33.5 2.2 %collective-permute-done.4 = bf16[32,2048]{1,0:T(8,128)(2,1)S(1)} collective-permute-done((bf16[32,2048]{1,0:T(8,128)(2,1)S(1)}, bf16[32,2048]{1,0:T(8,128)(2,1)S(1)}, u32[]{:S(2)}, u32[]{:S(2)}) %collective-permute-start.4) | collective-permute-done | bytes 131104 | tf_op jit(solution)/shard_map/ppermute | solution.py:229
  35.7 0.1 collective-permute-done.5
  35.8 0.7 %convert_add_fusion = f32[32,2048]{1,0:T(8,128)} fusion(bf16[32,2048]{1,0:T(8,128)(2,1)S(1)} %collective-permute-done.5, f32[32,2048]{1,0:T(8,128)S(1)} %get-tuple-element.15, bf16[32,2048]{1,0:T(8,128)(2,1)S(1)} %collective-permute-done.4), kind=kLoop, calls=%fused_computation | loop fusion | flops 262144 | bytes 786432 | tf_op jit(solution)/shard_map/add | solution.py:277
  (3 shorter events, 0.1 us)
Async XLA Ops:
  1.6 11.4 %collective-permute-start.1 = (bf16[32,2048]{1,0:T(8,128)(2,1)S(1)}, bf16[32,2048]{1,0:T(8,128)(2,1)S(1)}, u32[]{:S(2)}, u32[]{:S(2)}) collective-permute-start(bf16[32,2048]{1,0:T(8,128)(2,1)S(1)} %convert_element_type.12.grad_ref.upper_ref.refs_0_), channel_id=1, source_target_pairs={{2,0},{3,1},{0,2},{1,3},{6,4},{7,5},{4,6},{5,7},{10,8},{11,9},{8,1... | collective-permute-start | bytes 393224 | tf_op jit(solution)/shard_map/ppermute | solution.py:225
  5.7 0.9 %copy-start.4 = (f32[32,2048]{1,0:T(8,128)S(1)}, f32[32,2048]{1,0:T(8,128)}, u32[]{:S(2)}) copy-start(f32[32,2048]{1,0:T(8,128)} %lower_ref.1) | copy-start | bytes 786436
  6.7 6.8 %copy-start.5 = (f32[32,2048]{1,0:T(8,128)S(1)}, f32[32,2048]{1,0:T(8,128)}, u32[]{:S(2)}) copy-start(f32[32,2048]{1,0:T(8,128)} %lower_ref.1) | copy-start | bytes 786436
  6.7 12.4 %collective-permute-start = (bf16[64,2048]{1,0:T(8,128)(2,1)S(1)}, bf16[64,2048]{1,0:T(8,128)(2,1)S(1)}, u32[]{:S(2)}, u32[]{:S(2)}) collective-permute-start(bf16[64,2048]{1,0:T(8,128)(2,1)S(1)} %pair.1), channel_id=1, source_target_pairs={{1,0},{0,1},{3,2},{2,3},{5,4},{4,5},{7,6},{6,7},{9,8},{8,9},{11,10... | collective-permute-start | bytes 786440 | tf_op jit(solution)/shard_map/ppermute | solution.py:225
  8.3 1.4 %copy-start = (bf16[2048,384]{1,0:T(8,128)(2,1)S(1)}, bf16[2048,384]{1,0:T(8,128)(2,1)}, u32[]{:S(2)}) copy-start(bf16[2048,384]{1,0:T(8,128)(2,1)} %w_out_ref.3) | copy-start | bytes 4718596
  9.7 1.4 %copy-start.2 = (bf16[2048,384]{1,0:T(8,128)(2,1)S(1)}, bf16[2048,384]{1,0:T(8,128)(2,1)}, u32[]{:S(2)}) copy-start(bf16[2048,384]{1,0:T(8,128)(2,1)} %w_in_ref.3) | copy-start | bytes 4718596
  11.1 0.9 %copy-start.6 = (bf16[128,384]{1,0:T(8,128)(2,1)S(1)}, bf16[128,384]{1,0:T(8,128)(2,1)}, u32[]{:S(2)}) copy-start(bf16[128,384]{1,0:T(8,128)(2,1)} %pre_ref.4) | copy-start | bytes 294916
  12.0 9.4 %copy-start.1 = (bf16[2048,384]{1,0:T(8,128)(2,1)S(1)}, bf16[2048,384]{1,0:T(8,128)(2,1)}, u32[]{:S(2)}) copy-start(bf16[2048,384]{1,0:T(8,128)(2,1)} %w_out_ref.3) | copy-start | bytes 4718596
  12.0 9.4 %copy-start.3 = (bf16[2048,384]{1,0:T(8,128)(2,1)S(1)}, bf16[2048,384]{1,0:T(8,128)(2,1)}, u32[]{:S(2)}) copy-start(bf16[2048,384]{1,0:T(8,128)(2,1)} %w_in_ref.3) | copy-start | bytes 4718596
  13.0 8.5 %collective-permute-start.2 = (bf16[32,2048]{1,0:T(8,128)(2,1)S(1)}, bf16[32,2048]{1,0:T(8,128)(2,1)S(1)}, u32[]{:S(2)}, u32[]{:S(2)}) collective-permute-start(bf16[32,2048]{1,0:T(8,128)(2,1)S(1)} %collective-permute-done.1.refs_1_.refs_2_), channel_id=1, source_target_pairs={{1,0},{0,1},{3,2},{2,3},{5,4},{4,5},{7,6},{6,7},{9,8},{8,9},{11,10... | collective-permute-start | bytes 393224 | tf_op jit(solution)/shard_map/ppermute | solution.py:225
  13.5 10.5 %collective-permute-start.6 = (bf16[32,2048]{1,0:T(8,128)(2,1)S(1)}, bf16[32,2048]{1,0:T(8,128)(2,1)S(1)}, u32[]{:S(2)}, u32[]{:S(2)}) collective-permute-start(bf16[32,2048]{1,0:T(8,128)(2,1)S(1)} %convert_element_type.15.refs_0_), channel_id=1, source_target_pairs={{2,0},{3,1},{0,2},{1,3},{6,4},{7,5},{4,6},{5,7},{10,8},{11,9},{8,1... | collective-permute-start | bytes 393224 | tf_op jit(solution)/shard_map/ppermute | solution.py:225
  22.4 6.2 %collective-permute-start.3 = (bf16[32,2048]{1,0:T(8,128)(2,1)S(1)}, bf16[32,2048]{1,0:T(8,128)(2,1)S(1)}, u32[]{:S(2)}, u32[]{:S(2)}) collective-permute-start(bf16[32,2048]{1,0:T(8,128)(2,1)S(1)} %get-tuple-element.19), channel_id=1, source_target_pairs={{1,0},{0,1},{3,2},{2,3},{5,4},{4,5},{7,6},{6,7},{9,8},{8,9},{11,10... | collective-permute-start | bytes 393224 | tf_op jit(solution)/shard_map/ppermute | solution.py:225
  24.0 8.1 %collective-permute-start.7 = (bf16[32,2048]{1,0:T(8,128)(2,1)S(1)}, bf16[32,2048]{1,0:T(8,128)(2,1)S(1)}, u32[]{:S(2)}, u32[]{:S(2)}) collective-permute-start(bf16[32,2048]{1,0:T(8,128)(2,1)S(1)} %collective-permute-done.6.refs_2_), channel_id=1, source_target_pairs={{1,0},{0,1},{3,2},{2,3},{5,4},{4,5},{7,6},{6,7},{9,8},{8,9},{11,10... | collective-permute-start | bytes 393224 | tf_op jit(solution)/shard_map/ppermute | solution.py:225
  28.6 7.1 %collective-permute-start.4 = (bf16[32,2048]{1,0:T(8,128)(2,1)S(1)}, bf16[32,2048]{1,0:T(8,128)(2,1)S(1)}, u32[]{:S(2)}, u32[]{:S(2)}) collective-permute-start(bf16[32,2048]{1,0:T(8,128)(2,1)S(1)} %add.9), channel_id=1, source_target_pairs={{0,2},{1,3},{2,0},{3,1},{4,6},{5,7},{6,4},{7,5},{8,10},{9,11},{10,... | collective-permute-start | bytes 393224 | tf_op jit(solution)/shard_map/ppermute | solution.py:229
  29.0 6.8 %collective-permute-start.5 = (bf16[32,2048]{1,0:T(8,128)(2,1)S(1)}, bf16[32,2048]{1,0:T(8,128)(2,1)S(1)}, u32[]{:S(2)}, u32[]{:S(2)}) collective-permute-start(bf16[32,2048]{1,0:T(8,128)(2,1)S(1)} %get-tuple-element.22), channel_id=1, source_target_pairs={{1,0},{0,1},{3,2},{2,3},{5,4},{4,5},{7,6},{6,7},{9,8},{8,9},{11,10... | collective-permute-start | bytes 393224 | tf_op jit(solution)/shard_map/ppermute | solution.py:225

commit v2 on v1

--- a/solution.py
+++ b/solution.py
@@ -43,25 +43,6 @@
 
 def stack(refs, starts, rows, columns=slice(None)):
     return jnp.concatenate([ref[s : s + rows, columns] for ref, s in zip(refs, starts)], axis=0)
-
-
-def pair_kernel(upper_ref, lower_ref, both_ref):
-    rows = upper_ref.shape[0]
-    both_ref[:rows, :] = upper_ref[...]
-    both_ref[rows:, :] = lower_ref[...].astype(both_ref.dtype)
-
-
-def pair(upper, lower):
-    rows, width = upper.shape
-    return pl.pallas_call(
-        pair_kernel,
-        out_shape=jax.ShapeDtypeStruct((2 * rows, width), upper.dtype),
-        in_specs=[VMEM] * 2,
-        out_specs=VMEM,
-        cost_estimate=cost(0, 10 * rows * width),
-        compiler_params=PARAMS,
-        name="pair",
-    )(upper, lower)
 
 
 def share(pre, grads, w_out_ref, w_in_ref, emit):
@@ -81,31 +62,32 @@
     return hid
 
 
-def own_kernel(n, me_ref, pre_ref, w_out_ref, w_in_ref, grad_ref, hid_ref, part_ref):
-    rows = part_ref.shape[0]
+def own_kernel(n, me_ref, pre_ref, w_out_ref, w_in_ref, grad_ref, inputs_ref, narrow_ref, hid_ref, part_ref):
+    narrow_ref[...] = inputs_ref[...].astype(narrow_ref.dtype)
 
     def emit(columns, part):
         part_ref[:, columns] = part
 
-    pre = pre_block(pre_ref, me_ref[0], 0, n, rows)
+    pre = pre_block(pre_ref, me_ref[0], 0, n, grad_ref.shape[0])
     hid_ref[...] = share(pre, grad_ref[...], w_out_ref, w_in_ref, emit)
 
 
-def own_block(n, me, pre, w_out_t, w_in, grad):
-    hidden, width = pre.shape[1], w_in.shape[0]
-    rows = pre.shape[0] // n
+def own_block(n, me, pre, w_out_t, w_in, grad, inputs):
+    rows, width = grad.shape
+    hidden = pre.shape[1]
     return pl.pallas_call(
         functools.partial(own_kernel, n),
         out_shape=[
+            jax.ShapeDtypeStruct((rows, width), jnp.bfloat16),
             jax.ShapeDtypeStruct((rows, hidden), jnp.bfloat16),
             jax.ShapeDtypeStruct((rows, width), jnp.float32),
         ],
-        in_specs=[SMEM] + [VMEM] * 4,
-        out_specs=[VMEM] * 2,
-        cost_estimate=cost(4 * rows * width * hidden, 4 * width * hidden + 6 * rows * width),
+        in_specs=[SMEM] + [VMEM] * 5,
+        out_specs=[VMEM] * 3,
+        cost_estimate=cost(4 * rows * width * hidden, 4 * width * hidden + 12 * rows * width),
         compiler_params=PARAMS,
         name="own_block",
-    )(me, pre, w_out_t, w_in, grad)
+    )(me, pre, w_out_t, w_in, grad, inputs)
 
 
 def partial_kernel(n, starts, me_ref, pre_ref, w_out_ref, w_in_ref, *refs):
@@ -239,41 +221,36 @@
     rows = inputs.shape[0]
     me = lax.axis_index(AXIS).astype(jnp.int32).reshape(1)
     grad_bf = out_grad.astype(jnp.bfloat16)
-    far_grads = [from_slot(n, grad_bf, k) for k in far]
-    both = pair(grad_bf, inputs)
     grads, ins = {0: (grad_bf, 0)}, {}
+    for k in reversed(range(1, n)):
+        grads[k] = (from_slot(n, grad_bf, k), 0)
+    inputs_bf, own_hid, input_grad = own_block(n, me, pre_saved, w_out_t, w_in, grad_bf, inputs)
+    hids, ins[0] = [own_hid], (inputs_bf, 0)
+    near = from_slot(n, inputs_bf, 1) if team == 2 else inputs_bf
     if team == 2:
-        near = from_slot(n, both, 1)
-        grads[1], ins[1] = (near, 0), (near, rows)
-    own_hid, input_grad = own_block(n, me, pre_saved, w_out_t, w_in, grad_bf)
-    hids = [own_hid]
-    far_grads = later(far_grads, own_hid)
-    for k, got in zip(far, far_grads):
-        grads[k] = (got, 0)
+        ins[1] = (near, 0)
+    inputs_bf = later(inputs_bf, [grads[k][0] for k in range(1, n)])
+    for k in far:
+        got = from_slot(n, inputs_bf, k)
+        ins[k] = (got, 0)
         if team == 2:
-            grads[k + 1] = (from_slot(n, got, 1), 0)
-    inputs_bf = later(inputs, far_grads).astype(jnp.bfloat16)
-    ins[0] = (inputs_bf, 0)
-    far_ins = [from_slot(n, inputs_bf, k) for k in far]
-    arrived, pre = [], pre_saved
+            ins[k + 1] = (from_slot(n, got, 1), 0)
+    arrived = []
     if n > 1:
         hid, *parts = partials(n, me, pre_saved, w_out_t, w_in, [grads[k] for k in range(1, n)])
-        pre = later(pre, parts)
+        parts, near = lax.optimization_barrier((parts, near))
         parts = [None] + parts
         hids.append(hid)
+        if team == 2:
+            ins[1] = (near, 0)
         sums = [parts[k] + from_slot(n, parts[k + 1], 1) if team == 2 else parts[k] for k in far]
         sums, parts = lax.optimization_barrier((sums, parts))
         arrived = [to_slot(n, block, k) for k, block in zip(far, sums)]
         if team == 2:
             arrived.append(from_slot(n, parts[1], 1))
-    grad_w_out_t = out_weight_grad(n, me, [grads[k] for k in range(n)], pre)
-    far_ins = later(far_ins, grad_w_out_t)
-    for k, got in zip(far, far_ins):
-        ins[k] = (got, 0)
-        if team == 2:
-            ins[k + 1] = (from_slot(n, got, 1), 0)
+    grad_w_out_t = out_weight_grad(n, me, [grads[k] for k in range(n)], pre_saved)
     grad_w_in = in_weight_grad(n, [ins[k] for k in range(n)], hids)
-    for block in arrived:
+    for block in later(arrived, grad_w_in):
         input_grad = input_grad + block.astype(jnp.float32)
     return (input_grad, grad_w_in, grad_w_out_t)
 

time: 36.8 us -> 37.2 us (1.011)
  waiting for transfers between devices: 10.6 us -> 13.3 us
  starting transfers between devices: 14 us -> 11.7 us
    ppermute x7 -> x8, waiting for transfers between devices: 8.36 us -> 12.4 us  [from_slot(): lax.ppermute(block, AXIS, [(owner_of(i, slot, n), i) for i in range(n)])]
    ppermute x7 -> x8, starting transfers between devices: 13.7 us -> 11.6 us  [from_slot(): lax.ppermute(block, AXIS, [(owner_of(i, slot, n), i) for i in range(n)])]
    ppermute x1, waiting for transfers between devices: 2.21 us -> 0.9 us  [to_slot(): lax.ppermute(block, AXIS, [(i, owner_of(i, slot, n)) for i in range(n)])]
    unnamed x14 -> x8, local copies, waits for them, and re-layouts: 4.67 us -> 4.66 us
  transfers between devices with their start and end apart: 8 -> 9, of which waited for: 6 -> 6; matrix products, arithmetic and copies ran while one was open for 0% -> 0% of each run, Pallas kernels for 13% -> 13%
where the time goes in v2:
time: 37.2 us; the launch traced here: 36.9 us
  waiting for transfers between devices  13.3 us (36%)
  starting transfers between devices  11.7 us (31%)
  Pallas kernels  4.8 us (13%)
  local copies, waits for them, and re-layouts  4.66 us (13%)
  other arithmetic  1.74 us (5%)
  between operations  0.69 us (2%)
    ppermute x8, waiting for transfers between devices, from_slot(): lax.ppermute(block, AXIS, [(owner_of(i, slot, n), i) for i in range(n)])  12.4 us
    ppermute x8, starting transfers between devices, from_slot(): lax.ppermute(block, AXIS, [(owner_of(i, slot, n), i) for i in range(n)])  11.6 us
    unnamed x8, local copies, waits for them, and re-layouts  4.66 us
    pallas_call x1, Pallas kernels, out_weight_grad(): pl.pallas_call(functools.partial(out_kernel, n, starts), out_shape=jax.Sh...  1.46 us
    pallas_call x1, Pallas kernels, in_weight_grad(): pl.pallas_call(functools.partial(in_kernel, n, starts, len(hids)), out_sh...  1.46 us
    convert_element_type x1, other arithmetic, on_device(): grad_bf = out_grad.astype(jnp.bfloat16)  0.97 us
    pallas_call x1, Pallas kernels, partials(): pl.pallas_call(functools.partial(partial_kernel, n, starts), out_shape=[j...  0.95 us
    pallas_call x1, Pallas kernels, own_block(): pl.pallas_call(functools.partial(own_kernel, n), out_shape=[jax.ShapeDtyp...  0.93 us
  transfers between devices with their start and end apart: 9, of which 6 were waited for; matrix products, arithmetic and copies ran while one was open for 0% of the time, Pallas kernels for 13%

profile of v2, /device:TPU:0, one launch (start us, length us, event | category | flops | bytes accessed | tf_op | source)
XLA Modules:
  0.0 36.9 jit_solution(13870708270192394172)
XLA Ops:
  0.6 1.0 %convert_element_type.9.grad_ref.refs_0_ = bf16[32,2048]{1,0:T(8,128)(2,1)S(1)} convert(f32[32,2048]{1,0:T(8,128)} %param.6) | non-fusion elementwise | flops 65536 | bytes 393216 | tf_op jit(solution)/shard_map/convert_element_type | solution.py:223
  1.6 3.1 %collective-permute-start = (bf16[32,2048]{1,0:T(8,128)(2,1)S(1)}, bf16[32,2048]{1,0:T(8,128)(2,1)S(1)}, u32[]{:S(2)}, u32[]{:S(2)}) collective-permute-start(bf16[32,2048]{1,0:T(8,128)(2,1)S(1)} %convert_element_type.9.grad_ref.refs_0_), channel_id=1, source_target_pairs={{1,0},{0,1},{3,2},{2,3},{5,4},{4,5},{7,6},{6,7},{9,8},{8,9},{11,10... | collective-permute-start | bytes 393224 | tf_op jit(solution)/shard_map/ppermute | solution.py:207
  4.7 2.6 %collective-permute-start.1 = (bf16[32,2048]{1,0:T(8,128)(2,1)S(1)}, bf16[32,2048]{1,0:T(8,128)(2,1)S(1)}, u32[]{:S(2)}, u32[]{:S(2)}) collective-permute-start(bf16[32,2048]{1,0:T(8,128)(2,1)S(1)} %convert_element_type.9.grad_ref.refs_0_), channel_id=1, source_target_pairs={{2,0},{3,1},{0,2},{1,3},{6,4},{7,5},{4,6},{5,7},{10,8},{11,9},{8,1... | collective-permute-start | bytes 393224 | tf_op jit(solution)/shard_map/ppermute | solution.py:207
  7.3 0.0 collective-permute-start.2
  7.3 0.0 copy-start
  7.3 1.4 %copy-done = bf16[2048,384]{1,0:T(8,128)(2,1)S(1)} copy-done((bf16[2048,384]{1,0:T(8,128)(2,1)S(1)}, bf16[2048,384]{1,0:T(8,128)(2,1)}, u32[]{:S(2)}) %copy-start) | copy-done | bytes 1572888
  8.7 0.0 copy-start.1
  8.7 1.4 %copy-done.1 = bf16[2048,384]{1,0:T(8,128)(2,1)S(1)} copy-done((bf16[2048,384]{1,0:T(8,128)(2,1)S(1)}, bf16[2048,384]{1,0:T(8,128)(2,1)}, u32[]{:S(2)}) %copy-start.1) | copy-done | bytes 1572888
  10.1 0.0 copy-start.2
  10.1 0.9 %copy-done.2 = bf16[128,384]{1,0:T(8,128)(2,1)S(1)} copy-done((bf16[128,384]{1,0:T(8,128)(2,1)S(1)}, bf16[128,384]{1,0:T(8,128)(2,1)}, u32[]{:S(2)}) %copy-start.2) | copy-done | bytes 98328
  11.0 0.0 copy-start.3
  11.0 0.9 %copy-done.3 = f32[32,2048]{1,0:T(8,128)S(1)} copy-done((f32[32,2048]{1,0:T(8,128)S(1)}, f32[32,2048]{1,0:T(8,128)}, u32[]{:S(2)}) %copy-start.3) | copy-done | bytes 262168
  11.9 0.9 %own_block.1 = (bf16[32,2048]{1,0:T(8,128)(2,1)S(1)}, bf16[32,384]{1,0:T(8,128)(2,1)S(1)}, f32[32,2048]{1,0:T(8,128)S(1)}) custom-call(s32[1]{0:T(128)} %bitcast.me_ref, bf16[128,384]{1,0:T(8,128)(2,1)S(1)} %copy-done.2, bf16[2048,384]{1,0:T(8,128)(2,1)S(1)} %copy-done, bf16[2048,384]{1,0:T(8,128)(2,1)S(1)} %copy-done.1, ...), custom_call_target="tpu_custom_call" | custom-call | flops 100663296 | bytes 3932160 | tf_op jit(solution)/shard_map/own_block/pallas_call | solution.py:78
  12.9 0.9 %collective-permute-start.3 = (bf16[32,2048]{1,0:T(8,128)(2,1)S(1)}, bf16[32,2048]{1,0:T(8,128)(2,1)S(1)}, u32[]{:S(2)}, u32[]{:S(2)}) collective-permute-start(bf16[32,2048]{1,0:T(8,128)(2,1)S(1)} %get-tuple-element.30.refs_0_), channel_id=1, source_target_pairs={{1,0},{0,1},{3,2},{2,3},{5,4},{4,5},{7,6},{6,7},{9,8},{8,9},{11,10... | collective-permute-start | bytes 393224 | tf_op jit(solution)/shard_map/ppermute | solution.py:207
  13.8 0.0 collective-permute-done.refs_0_.refs_1_
  13.8 3.8 %collective-permute-done.1.refs_1_.refs_2_ = bf16[32,2048]{1,0:T(8,128)(2,1)S(1)} collective-permute-done((bf16[32,2048]{1,0:T(8,128)(2,1)S(1)}, bf16[32,2048]{1,0:T(8,128)(2,1)S(1)}, u32[]{:S(2)}, u32[]{:S(2)}) %collective-permute-start.1) | collective-permute-done | bytes 131104 | tf_op jit(solution)/shard_map/ppermute | solution.py:207
  17.6 0.0 collective-permute-done.2.refs_2_.refs_3_
  17.6 3.0 %collective-permute-start.7 = (bf16[32,2048]{1,0:T(8,128)(2,1)S(1)}, bf16[32,2048]{1,0:T(8,128)(2,1)S(1)}, u32[]{:S(2)}, u32[]{:S(2)}) collective-permute-start(bf16[32,2048]{1,0:T(8,128)(2,1)S(1)} %get-tuple-element.30.refs_0_), channel_id=1, source_target_pairs={{2,0},{3,1},{0,2},{1,3},{6,4},{7,5},{4,6},{5,7},{10,8},{11,9},{8,1... | collective-permute-start | bytes 393224 | tf_op jit(solution)/shard_map/ppermute | solution.py:207
  20.6 1.0 %partials.1 = (bf16[96,384]{1,0:T(8,128)(2,1)S(1)}, bf16[32,2048]{1,0:T(8,128)(2,1)S(1)}, bf16[32,2048]{1,0:T(8,128)(2,1)S(1)}, bf16[32,2048]{1,0:T(8,128)(2,1)S(1)}) custom-call(s32[1]{0:T(128)} %bitcast.me_ref, bf16[128,384]{1,0:T(8,128)(2,1)S(1)} %copy-done.2, bf16[2048,384]{1,0:T(8,128)(2,1)S(1)} %copy-done, bf16[2048,384]{1,0:T(8,128)(2,1)S(1)} %copy-done.1, ...), custom_call_target="tpu_custom_call" | custom-call | flops 301989888 | bytes 4079616 | tf_op jit(solution)/shard_map/partials/pallas_call | solution.py:112
  21.5 0.0 collective-permute-done.3.refs_1_
  21.6 0.1 collective-permute-start.4
  21.6 4.4 %collective-permute-done.7.refs_2_ = bf16[32,2048]{1,0:T(8,128)(2,1)S(1)} collective-permute-done((bf16[32,2048]{1,0:T(8,128)(2,1)S(1)}, bf16[32,2048]{1,0:T(8,128)(2,1)S(1)}, u32[]{:S(2)}, u32[]{:S(2)}) %collective-permute-start.7) | collective-permute-done | bytes 131104 | tf_op jit(solution)/shard_map/ppermute | solution.py:207
  26.0 0.1 collective-permute-start.8
  26.1 2.3 %collective-permute-done.4 = bf16[32,2048]{1,0:T(8,128)(2,1)S(1)} collective-permute-done((bf16[32,2048]{1,0:T(8,128)(2,1)S(1)}, bf16[32,2048]{1,0:T(8,128)(2,1)S(1)}, u32[]{:S(2)}, u32[]{:S(2)}) %collective-permute-start.4) | collective-permute-done | bytes 131104 | tf_op jit(solution)/shard_map/ppermute | solution.py:207
  28.5 0.1 collective-permute-start.5
  28.6 1.9 %collective-permute-start.6 = (bf16[32,2048]{1,0:T(8,128)(2,1)S(1)}, bf16[32,2048]{1,0:T(8,128)(2,1)S(1)}, u32[]{:S(2)}, u32[]{:S(2)}) collective-permute-start(bf16[32,2048]{1,0:T(8,128)(2,1)S(1)} %get-tuple-element.28), channel_id=1, source_target_pairs={{1,0},{0,1},{3,2},{2,3},{5,4},{4,5},{7,6},{6,7},{9,8},{8,9},{11,10... | collective-permute-start | bytes 393224 | tf_op jit(solution)/shard_map/ppermute | solution.py:207
  30.4 1.5 %out_weight_grad.1 = bf16[2048,384]{1,0:T(8,128)(2,1)} custom-call(s32[1]{0:T(128)} %bitcast.me_ref, bf16[128,384]{1,0:T(8,128)(2,1)S(1)} %copy-done.2, bf16[32,2048]{1,0:T(8,128)(2,1)S(1)} %convert_element_type.9.grad_ref.refs_0_, bf16[32,2048]{1,0:T(8,128)(2,1)S(1)} %collective-permute-done.refs_0_.refs_1_, ...), custom_call_target="tpu_custom_call" | custom-call | flops 201326592 | bytes 2195456 | tf_op jit(solution)/shard_map/out_weight_grad/pallas_call | solution.py:174
  31.9 1.6 %collective-permute-done.8.refs_3_ = bf16[32,2048]{1,0:T(8,128)(2,1)S(1)} collective-permute-done((bf16[32,2048]{1,0:T(8,128)(2,1)S(1)}, bf16[32,2048]{1,0:T(8,128)(2,1)S(1)}, u32[]{:S(2)}, u32[]{:S(2)}) %collective-permute-start.8) | collective-permute-done | bytes 131104 | tf_op jit(solution)/shard_map/ppermute | solution.py:207
  33.5 1.5 %in_weight_grad.1 = bf16[2048,384]{1,0:T(8,128)(2,1)} custom-call(bf16[32,2048]{1,0:T(8,128)(2,1)S(1)} %get-tuple-element.30.refs_0_, bf16[32,2048]{1,0:T(8,128)(2,1)S(1)} %collective-permute-done.3.refs_1_, bf16[32,2048]{1,0:T(8,128)(2,1)S(1)} %collective-permute-done.7.refs_2_, bf16[32,2048]{1,0:T(8,128)(2,1)S(1)} %collective-permute-done.8.refs_3_, ...), custom_call_target="tpu_custom_call" | custom-call | flops 201326592 | bytes 2195456 | tf_op jit(solution)/shard_map/in_weight_grad/pallas_call | solution.py:189
  35.0 0.9 %collective-permute-done.5 = bf16[32,2048]{1,0:T(8,128)(2,1)S(1)} collective-permute-done((bf16[32,2048]{1,0:T(8,128)(2,1)S(1)}, bf16[32,2048]{1,0:T(8,128)(2,1)S(1)}, u32[]{:S(2)}, u32[]{:S(2)}) %collective-permute-start.5) | collective-permute-done | bytes 131104 | tf_op jit(solution)/shard_map/ppermute | solution.py:211
  35.9 0.3 collective-permute-done.6
  36.2 0.7 %convert_add_fusion = f32[32,2048]{1,0:T(8,128)} fusion(bf16[32,2048]{1,0:T(8,128)(2,1)S(1)} %collective-permute-done.6, f32[32,2048]{1,0:T(8,128)S(1)} %get-tuple-element.19, bf16[32,2048]{1,0:T(8,128)(2,1)S(1)} %collective-permute-done.5), kind=kLoop, calls=%fused_computation | loop fusion | flops 262144 | bytes 786432 | tf_op jit(solution)/shard_map/add | solution.py:254
  (1 shorter events, 0.0 us)
Async XLA Ops:
  1.6 12.2 %collective-permute-start = (bf16[32,2048]{1,0:T(8,128)(2,1)S(1)}, bf16[32,2048]{1,0:T(8,128)(2,1)S(1)}, u32[]{:S(2)}, u32[]{:S(2)}) collective-permute-start(bf16[32,2048]{1,0:T(8,128)(2,1)S(1)} %convert_element_type.9.grad_ref.refs_0_), channel_id=1, source_target_pairs={{1,0},{0,1},{3,2},{2,3},{5,4},{4,5},{7,6},{6,7},{9,8},{8,9},{11,10... | collective-permute-start | bytes 393224 | tf_op jit(solution)/shard_map/ppermute | solution.py:207
  4.7 12.9 %collective-permute-start.1 = (bf16[32,2048]{1,0:T(8,128)(2,1)S(1)}, bf16[32,2048]{1,0:T(8,128)(2,1)S(1)}, u32[]{:S(2)}, u32[]{:S(2)}) collective-permute-start(bf16[32,2048]{1,0:T(8,128)(2,1)S(1)} %convert_element_type.9.grad_ref.refs_0_), channel_id=1, source_target_pairs={{2,0},{3,1},{0,2},{1,3},{6,4},{7,5},{4,6},{5,7},{10,8},{11,9},{8,1... | collective-permute-start | bytes 393224 | tf_op jit(solution)/shard_map/ppermute | solution.py:207
  7.3 10.3 %collective-permute-start.2 = (bf16[32,2048]{1,0:T(8,128)(2,1)S(1)}, bf16[32,2048]{1,0:T(8,128)(2,1)S(1)}, u32[]{:S(2)}, u32[]{:S(2)}) collective-permute-start(bf16[32,2048]{1,0:T(8,128)(2,1)S(1)} %convert_element_type.9.grad_ref.refs_0_), channel_id=1, source_target_pairs={{3,0},{2,1},{1,2},{0,3},{7,4},{6,5},{5,6},{4,7},{11,8},{10,9},{9,1... | collective-permute-start | bytes 393224 | tf_op jit(solution)/shard_map/ppermute | solution.py:207
  7.3 1.4 %copy-start = (bf16[2048,384]{1,0:T(8,128)(2,1)S(1)}, bf16[2048,384]{1,0:T(8,128)(2,1)}, u32[]{:S(2)}) copy-start(bf16[2048,384]{1,0:T(8,128)(2,1)} %w_out_ref.3) | copy-start | bytes 4718596
  8.7 1.4 %copy-start.1 = (bf16[2048,384]{1,0:T(8,128)(2,1)S(1)}, bf16[2048,384]{1,0:T(8,128)(2,1)}, u32[]{:S(2)}) copy-start(bf16[2048,384]{1,0:T(8,128)(2,1)} %w_in_ref.3) | copy-start | bytes 4718596
  10.1 0.9 %copy-start.2 = (bf16[128,384]{1,0:T(8,128)(2,1)S(1)}, bf16[128,384]{1,0:T(8,128)(2,1)}, u32[]{:S(2)}) copy-start(bf16[128,384]{1,0:T(8,128)(2,1)} %pre_ref.5) | copy-start | bytes 294916
  11.0 0.9 %copy-start.3 = (f32[32,2048]{1,0:T(8,128)S(1)}, f32[32,2048]{1,0:T(8,128)}, u32[]{:S(2)}) copy-start(f32[32,2048]{1,0:T(8,128)} %inputs_ref.1) | copy-start | bytes 786436
  12.9 8.7 %collective-permute-start.3 = (bf16[32,2048]{1,0:T(8,128)(2,1)S(1)}, bf16[32,2048]{1,0:T(8,128)(2,1)S(1)}, u32[]{:S(2)}, u32[]{:S(2)}) collective-permute-start(bf16[32,2048]{1,0:T(8,128)(2,1)S(1)} %get-tuple-element.30.refs_0_), channel_id=1, source_target_pairs={{1,0},{0,1},{3,2},{2,3},{5,4},{4,5},{7,6},{6,7},{9,8},{8,9},{11,10... | collective-permute-start | bytes 393224 | tf_op jit(solution)/shard_map/ppermute | solution.py:207
  17.6 8.4 %collective-permute-start.7 = (bf16[32,2048]{1,0:T(8,128)(2,1)S(1)}, bf16[32,2048]{1,0:T(8,128)(2,1)S(1)}, u32[]{:S(2)}, u32[]{:S(2)}) collective-permute-start(bf16[32,2048]{1,0:T(8,128)(2,1)S(1)} %get-tuple-element.30.refs_0_), channel_id=1, source_target_pairs={{2,0},{3,1},{0,2},{1,3},{6,4},{7,5},{4,6},{5,7},{10,8},{11,9},{8,1... | collective-permute-start | bytes 393224 | tf_op jit(solution)/shard_map/ppermute | solution.py:207
  21.6 6.9 %collective-permute-start.4 = (bf16[32,2048]{1,0:T(8,128)(2,1)S(1)}, bf16[32,2048]{1,0:T(8,128)(2,1)S(1)}, u32[]{:S(2)}, u32[]{:S(2)}) collective-permute-start(bf16[32,2048]{1,0:T(8,128)(2,1)S(1)} %get-tuple-element.25), channel_id=1, source_target_pairs={{1,0},{0,1},{3,2},{2,3},{5,4},{4,5},{7,6},{6,7},{9,8},{8,9},{11,10... | collective-permute-start | bytes 393224 | tf_op jit(solution)/shard_map/ppermute | solution.py:207
  26.0 7.4 %collective-permute-start.8 = (bf16[32,2048]{1,0:T(8,128)(2,1)S(1)}, bf16[32,2048]{1,0:T(8,128)(2,1)S(1)}, u32[]{:S(2)}, u32[]{:S(2)}) collective-permute-start(bf16[32,2048]{1,0:T(8,128)(2,1)S(1)} %collective-permute-done.7.refs_2_), channel_id=1, source_target_pairs={{1,0},{0,1},{3,2},{2,3},{5,4},{4,5},{7,6},{6,7},{9,8},{8,9},{11,10... | collective-permute-start | bytes 393224 | tf_op jit(solution)/shard_map/ppermute | solution.py:207
  28.5 7.4 %collective-permute-start.5 = (bf16[32,2048]{1,0:T(8,128)(2,1)S(1)}, bf16[32,2048]{1,0:T(8,128)(2,1)S(1)}, u32[]{:S(2)}, u32[]{:S(2)}) collective-permute-start(bf16[32,2048]{1,0:T(8,128)(2,1)S(1)} %add.9), channel_id=1, source_target_pairs={{0,2},{1,3},{2,0},{3,1},{4,6},{5,7},{6,4},{7,5},{8,10},{9,11},{10,... | collective-permute-start | bytes 393224 | tf_op jit(solution)/shard_map/ppermute | solution.py:211
  28.6 7.6 %collective-permute-start.6 = (bf16[32,2048]{1,0:T(8,128)(2,1)S(1)}, bf16[32,2048]{1,0:T(8,128)(2,1)S(1)}, u32[]{:S(2)}, u32[]{:S(2)}) collective-permute-start(bf16[32,2048]{1,0:T(8,128)(2,1)S(1)} %get-tuple-element.28), channel_id=1, source_target_pairs={{1,0},{0,1},{3,2},{2,3},{5,4},{4,5},{7,6},{6,7},{9,8},{8,9},{11,10... | collective-permute-start | bytes 393224 | tf_op jit(solution)/shard_map/ppermute | solution.py:207

commit v3 on v1

--- a/solution.py
+++ b/solution.py
@@ -214,6 +214,39 @@
         compiler_params=PARAMS,
         name="in_weight_grad",
     )(*lefts, *hids)
+
+
+def sum_kernel(part_ref, *refs):
+    arrived_refs, (sum_hbm, buffer, sems) = refs[:-3], refs[-3:]
+    tile = buffer.shape[1] // sems.shape[0]
+    moves = []
+    for k in range(sems.shape[0]):
+        columns = slice(k * tile, (k + 1) * tile)
+        total = part_ref[:, columns]
+        for ref in arrived_refs:
+            total = total + ref[:, columns].astype(jnp.float32)
+        buffer[:, columns] = total
+        moves.append(pltpu.make_async_copy(buffer.at[:, columns], sum_hbm.at[:, columns], sems.at[k]))
+        moves[k].start()
+    for move in moves:
+        move.wait()
+
+
+def summed(part, arrived):
+    rows, width = part.shape
+    return pl.pallas_call(
+        sum_kernel,
+        out_shape=jax.ShapeDtypeStruct(part.shape, jnp.float32),
+        in_specs=[VMEM] * (1 + len(arrived)),
+        out_specs=HBM,
+        scratch_shapes=[
+            pltpu.VMEM(part.shape, jnp.float32),
+            pltpu.SemaphoreType.DMA((width // largest_tile(width, 512),)),
+        ],
+        cost_estimate=cost(len(arrived) * rows * width, (8 + 2 * len(arrived)) * rows * width),
+        compiler_params=PARAMS,
+        name="sum",
+    )(part, *arrived)
 
 
 def owner_of(me, slot, n):
@@ -273,9 +306,7 @@
         if team == 2:
             ins[k + 1] = (from_slot(n, got, 1), 0)
     grad_w_in = in_weight_grad(n, [ins[k] for k in range(n)], hids)
-    for block in arrived:
-        input_grad = input_grad + block.astype(jnp.float32)
-    return (input_grad, grad_w_in, grad_w_out_t)
+    return (summed(input_grad, arrived), grad_w_in, grad_w_out_t)
 
 
 def solution(mesh):

time: 36.8 us -> 36.8 us (level)
  other arithmetic: 1.75 us -> 1.01 us
  Pallas kernels: 4.83 us -> 5.56 us
    pallas_call x0 -> x1, Pallas kernels: none -> 0.74 us  [summed(): pl.pallas_call(sum_kernel, out_shape=jax.ShapeDtypeStruct(part.shape, jnp...]
    add x1 -> x0, other arithmetic: 0.74 us -> none  [on_device(): input_grad = input_grad + block.astype(jnp.float32)]
    unnamed x14 -> x10, local copies, waits for them, and re-layouts: 4.67 us -> 4.66 us
where the time goes in v3:
time: 36.8 us; the launch traced here: 36.5 us
  starting transfers between devices  14 us (38%)
  waiting for transfers between devices  10.6 us (29%)
  Pallas kernels  5.56 us (15%)
  local copies, waits for them, and re-layouts  4.66 us (13%)
  other arithmetic  1.01 us (3%)
  between operations  0.69 us (2%)
    ppermute x7, starting transfers between devices, from_slot(): lax.ppermute(block, AXIS, [(owner_of(i, slot, n), i) for i in range(n)])  13.7 us
    ppermute x7, waiting for transfers between devices, from_slot(): lax.ppermute(block, AXIS, [(owner_of(i, slot, n), i) for i in range(n)])  8.38 us
    unnamed x10, local copies, waits for them, and re-layouts  4.66 us
    ppermute x1, waiting for transfers between devices, to_slot(): lax.ppermute(block, AXIS, [(i, owner_of(i, slot, n)) for i in range(n)])  2.21 us
    pallas_call x1, Pallas kernels, out_weight_grad(): pl.pallas_call(functools.partial(out_kernel, n, starts), out_shape=jax.Sh...  1.47 us
    pallas_call x1, Pallas kernels, in_weight_grad(): pl.pallas_call(functools.partial(in_kernel, n, starts, len(hids)), out_sh...  1.46 us
    convert_element_type x1, other arithmetic, on_device(): grad_bf = out_grad.astype(jnp.bfloat16)  0.97 us
    pallas_call x1, Pallas kernels, partials(): pl.pallas_call(functools.partial(partial_kernel, n, starts), out_shape=[j...  0.95 us
  transfers between devices with their start and end apart: 8, of which 6 were waited for; matrix products, arithmetic and copies ran while one was open for 0% of the time, Pallas kernels for 13%

profile of v3, /device:TPU:0, one launch (start us, length us, event | category | flops | bytes accessed | tf_op | source)
XLA Modules:
  0.0 36.5 jit_solution(8289070915125829955)
XLA Ops:
  0.6 1.0 %convert_element_type.6.grad_ref.upper_ref.refs_0_ = bf16[32,2048]{1,0:T(8,128)(2,1)S(1)} convert(f32[32,2048]{1,0:T(8,128)} %param.6) | non-fusion elementwise | flops 65536 | bytes 393216 | tf_op jit(solution)/shard_map/convert_element_type | solution.py:274
  1.6 4.1 %collective-permute-start.1 = (bf16[32,2048]{1,0:T(8,128)(2,1)S(1)}, bf16[32,2048]{1,0:T(8,128)(2,1)S(1)}, u32[]{:S(2)}, u32[]{:S(2)}) collective-permute-start(bf16[32,2048]{1,0:T(8,128)(2,1)S(1)} %convert_element_type.6.grad_ref.upper_ref.refs_0_), channel_id=1, source_target_pairs={{2,0},{3,1},{0,2},{1,3},{6,4},{7,5},{4,6},{5,7},{10,8},{11,9},{8,1... | collective-permute-start | bytes 393224 | tf_op jit(solution)/shard_map/ppermute | solution.py:258
  5.7 0.0 copy-start.2
  5.7 0.9 %copy-done.2 = f32[32,2048]{1,0:T(8,128)S(1)} copy-done((f32[32,2048]{1,0:T(8,128)S(1)}, f32[32,2048]{1,0:T(8,128)}, u32[]{:S(2)}) %copy-start.2) | copy-done | bytes 262168
  6.7 1.6 %collective-permute-start = (bf16[64,2048]{1,0:T(8,128)(2,1)S(1)}, bf16[64,2048]{1,0:T(8,128)(2,1)S(1)}, u32[]{:S(2)}, u32[]{:S(2)}) collective-permute-start(bf16[64,2048]{1,0:T(8,128)(2,1)S(1)} %pair.1), channel_id=1, source_target_pairs={{1,0},{0,1},{3,2},{2,3},{5,4},{4,5},{7,6},{6,7},{9,8},{8,9},{11,10... | collective-permute-start | bytes 786440 | tf_op jit(solution)/shard_map/ppermute | solution.py:258
  8.3 0.0 copy-start
  8.3 1.4 %copy-done = bf16[2048,384]{1,0:T(8,128)(2,1)S(1)} copy-done((bf16[2048,384]{1,0:T(8,128)(2,1)S(1)}, bf16[2048,384]{1,0:T(8,128)(2,1)}, u32[]{:S(2)}) %copy-start) | copy-done | bytes 1572888
  9.7 0.0 copy-start.1
  9.7 1.4 %copy-done.1 = bf16[2048,384]{1,0:T(8,128)(2,1)S(1)} copy-done((bf16[2048,384]{1,0:T(8,128)(2,1)S(1)}, bf16[2048,384]{1,0:T(8,128)(2,1)}, u32[]{:S(2)}) %copy-start.1) | copy-done | bytes 1572888
  11.1 0.0 copy-start.4
  11.1 0.9 %copy-done.4 = bf16[128,384]{1,0:T(8,128)(2,1)S(1)} copy-done((bf16[128,384]{1,0:T(8,128)(2,1)S(1)}, bf16[128,384]{1,0:T(8,128)(2,1)}, u32[]{:S(2)}) %copy-start.4) | copy-done | bytes 98328
  12.0 0.0 copy-start.3
  12.0 0.9 %own_block.1 = (bf16[32,384]{1,0:T(8,128)(2,1)S(1)}, f32[32,2048]{1,0:T(8,128)S(1)}) custom-call(s32[1]{0:T(128)} %bitcast.me_ref, bf16[128,384]{1,0:T(8,128)(2,1)S(1)} %copy-done.4, bf16[2048,384]{1,0:T(8,128)(2,1)S(1)} %copy-done, bf16[2048,384]{1,0:T(8,128)(2,1)S(1)} %copy-done.1, bf16[32,2048]{1,0:T(8,128)(2,1)S(1)} %convert_element_type.6.grad_ref.upper_ref.refs_0_), custom_call_target="tpu_custom_call" | custom-call | flops 100663296 | bytes 3538944 | tf_op jit(solution)/shard_map/own_block/pallas_call | solution.py:97
  13.0 0.0 collective-permute-done.1.refs_1_.refs_2_
  13.0 0.5 %collective-permute-start.2 = (bf16[32,2048]{1,0:T(8,128)(2,1)S(1)}, bf16[32,2048]{1,0:T(8,128)(2,1)S(1)}, u32[]{:S(2)}, u32[]{:S(2)}) collective-permute-start(bf16[32,2048]{1,0:T(8,128)(2,1)S(1)} %collective-permute-done.1.refs_1_.refs_2_), channel_id=1, source_target_pairs={{1,0},{0,1},{3,2},{2,3},{5,4},{4,5},{7,6},{6,7},{9,8},{8,9},{11,10... | collective-permute-start | bytes 393224 | tf_op jit(solution)/shard_map/ppermute | solution.py:258
  13.4 0.0 copy-done.3
  13.5 2.8 %collective-permute-start.6 = (bf16[32,2048]{1,0:T(8,128)(2,1)S(1)}, bf16[32,2048]{1,0:T(8,128)(2,1)S(1)}, u32[]{:S(2)}, u32[]{:S(2)}) collective-permute-start(bf16[32,2048]{1,0:T(8,128)(2,1)S(1)} %convert_element_type.7.refs_0_), channel_id=1, source_target_pairs={{2,0},{3,1},{0,2},{1,3},{6,4},{7,5},{4,6},{5,7},{10,8},{11,9},{8,1... | collective-permute-start | bytes 393224 | tf_op jit(solution)/shard_map/ppermute | solution.py:258
  16.3 2.8 %collective-permute-done.refs_0_.refs_1_ = bf16[64,2048]{1,0:T(8,128)(2,1)S(1)} collective-permute-done((bf16[64,2048]{1,0:T(8,128)(2,1)S(1)}, bf16[64,2048]{1,0:T(8,128)(2,1)S(1)}, u32[]{:S(2)}, u32[]{:S(2)}) %collective-permute-start) | collective-permute-done | bytes 262176 | tf_op jit(solution)/shard_map/ppermute | solution.py:258
  19.1 2.4 %collective-permute-done.2.refs_2_.refs_3_ = bf16[32,2048]{1,0:T(8,128)(2,1)S(1)} collective-permute-done((bf16[32,2048]{1,0:T(8,128)(2,1)S(1)}, bf16[32,2048]{1,0:T(8,128)(2,1)S(1)}, u32[]{:S(2)}, u32[]{:S(2)}) %collective-permute-start.2) | collective-permute-done | bytes 131104 | tf_op jit(solution)/shard_map/ppermute | solution.py:258
  21.5 1.0 %partials.1 = (bf16[96,384]{1,0:T(8,128)(2,1)S(1)}, bf16[32,2048]{1,0:T(8,128)(2,1)S(1)}, bf16[32,2048]{1,0:T(8,128)(2,1)S(1)}, bf16[32,2048]{1,0:T(8,128)(2,1)S(1)}) custom-call(s32[1]{0:T(128)} %bitcast.me_ref, bf16[128,384]{1,0:T(8,128)(2,1)S(1)} %copy-done.4, bf16[2048,384]{1,0:T(8,128)(2,1)S(1)} %copy-done, bf16[2048,384]{1,0:T(8,128)(2,1)S(1)} %copy-done.1, ...), custom_call_target="tpu_custom_call" | custom-call | flops 301989888 | bytes 4079616 | tf_op jit(solution)/shard_map/partials/pallas_call | solution.py:130
  22.4 0.1 collective-permute-start.3
  22.5 1.5 %out_weight_grad.1 = bf16[2048,384]{1,0:T(8,128)(2,1)} custom-call(s32[1]{0:T(128)} %bitcast.me_ref, bf16[128,384]{1,0:T(8,128)(2,1)S(1)} %copy-done.4, bf16[32,2048]{1,0:T(8,128)(2,1)S(1)} %convert_element_type.6.grad_ref.upper_ref.refs_0_, bf16[64,2048]{1,0:T(8,128)(2,1)S(1)} %collective-permute-done.refs_0_.refs_1_, ...), custom_call_target="tpu_custom_call" | custom-call | flops 201326592 | bytes 2195456 | tf_op jit(solution)/shard_map/out_weight_grad/pallas_call | solution.py:192
  24.0 0.0 collective-permute-done.6.refs_2_
  24.0 2.1 %collective-permute-start.7 = (bf16[32,2048]{1,0:T(8,128)(2,1)S(1)}, bf16[32,2048]{1,0:T(8,128)(2,1)S(1)}, u32[]{:S(2)}, u32[]{:S(2)}) collective-permute-start(bf16[32,2048]{1,0:T(8,128)(2,1)S(1)} %collective-permute-done.6.refs_2_), channel_id=1, source_target_pairs={{1,0},{0,1},{3,2},{2,3},{5,4},{4,5},{7,6},{6,7},{9,8},{8,9},{11,10... | collective-permute-start | bytes 393224 | tf_op jit(solution)/shard_map/ppermute | solution.py:258
  26.0 2.5 %collective-permute-done.3 = bf16[32,2048]{1,0:T(8,128)(2,1)S(1)} collective-permute-done((bf16[32,2048]{1,0:T(8,128)(2,1)S(1)}, bf16[32,2048]{1,0:T(8,128)(2,1)S(1)}, u32[]{:S(2)}, u32[]{:S(2)}) %collective-permute-start.3) | collective-permute-done | bytes 131104 | tf_op jit(solution)/shard_map/ppermute | solution.py:258
  28.6 0.3 collective-permute-start.4
  29.0 2.5 %collective-permute-start.5 = (bf16[32,2048]{1,0:T(8,128)(2,1)S(1)}, bf16[32,2048]{1,0:T(8,128)(2,1)S(1)}, u32[]{:S(2)}, u32[]{:S(2)}) collective-permute-start(bf16[32,2048]{1,0:T(8,128)(2,1)S(1)} %get-tuple-element.22), channel_id=1, source_target_pairs={{1,0},{0,1},{3,2},{2,3},{5,4},{4,5},{7,6},{6,7},{9,8},{8,9},{11,10... | collective-permute-start | bytes 393224 | tf_op jit(solution)/shard_map/ppermute | solution.py:258
  31.4 0.6 %collective-permute-done.7.refs_3_ = bf16[32,2048]{1,0:T(8,128)(2,1)S(1)} collective-permute-done((bf16[32,2048]{1,0:T(8,128)(2,1)S(1)}, bf16[32,2048]{1,0:T(8,128)(2,1)S(1)}, u32[]{:S(2)}, u32[]{:S(2)}) %collective-permute-start.7) | collective-permute-done | bytes 131104 | tf_op jit(solution)/shard_map/ppermute | solution.py:258
  32.0 1.5 %in_weight_grad.1 = bf16[2048,384]{1,0:T(8,128)(2,1)} custom-call(bf16[32,2048]{1,0:T(8,128)(2,1)S(1)} %convert_element_type.7.refs_0_, bf16[64,2048]{1,0:T(8,128)(2,1)S(1)} %collective-permute-done.refs_0_.refs_1_, bf16[32,2048]{1,0:T(8,128)(2,1)S(1)} %collective-permute-done.6.refs_2_, bf16[32,2048]{1,0:T(8,128)(2,1)S(1)} %collective-permute-done.7.refs_3_, ...), custom_call_target="tpu_custom_call" | custom-call | flops 201326592 | bytes 2195456 | tf_op jit(solution)/shard_map/in_weight_grad/pallas_call | solution.py:207
  33.5 2.2 %collective-permute-done.4.refs_0_ = bf16[32,2048]{1,0:T(8,128)(2,1)S(1)} collective-permute-done((bf16[32,2048]{1,0:T(8,128)(2,1)S(1)}, bf16[32,2048]{1,0:T(8,128)(2,1)S(1)}, u32[]{:S(2)}, u32[]{:S(2)}) %collective-permute-start.4) | collective-permute-done | bytes 131104 | tf_op jit(solution)/shard_map/ppermute | solution.py:262
  35.7 0.1 collective-permute-done.5.refs_1_
  35.8 0.7 %sum.1 = f32[32,2048]{1,0:T(8,128)} custom-call(f32[32,2048]{1,0:T(8,128)S(1)} %get-tuple-element.15.part_ref, bf16[32,2048]{1,0:T(8,128)(2,1)S(1)} %collective-permute-done.4.refs_0_, bf16[32,2048]{1,0:T(8,128)(2,1)S(1)} %collective-permute-done.5.refs_1_), custom_call_target="tpu_custom_call" | custom-call | flops 131072 | bytes 786432 | tf_op jit(solution)/shard_map/sum/pallas_call | solution.py:237
  (3 shorter events, 0.1 us)
Async XLA Ops:
  1.6 11.4 %collective-permute-start.1 = (bf16[32,2048]{1,0:T(8,128)(2,1)S(1)}, bf16[32,2048]{1,0:T(8,128)(2,1)S(1)}, u32[]{:S(2)}, u32[]{:S(2)}) collective-permute-start(bf16[32,2048]{1,0:T(8,128)(2,1)S(1)} %convert_element_type.6.grad_ref.upper_ref.refs_0_), channel_id=1, source_target_pairs={{2,0},{3,1},{0,2},{1,3},{6,4},{7,5},{4,6},{5,7},{10,8},{11,9},{8,1... | collective-permute-start | bytes 393224 | tf_op jit(solution)/shard_map/ppermute | solution.py:258
  5.7 0.9 %copy-start.2 = (f32[32,2048]{1,0:T(8,128)S(1)}, f32[32,2048]{1,0:T(8,128)}, u32[]{:S(2)}) copy-start(f32[32,2048]{1,0:T(8,128)} %lower_ref.1) | copy-start | bytes 786436
  6.7 12.4 %collective-permute-start = (bf16[64,2048]{1,0:T(8,128)(2,1)S(1)}, bf16[64,2048]{1,0:T(8,128)(2,1)S(1)}, u32[]{:S(2)}, u32[]{:S(2)}) collective-permute-start(bf16[64,2048]{1,0:T(8,128)(2,1)S(1)} %pair.1), channel_id=1, source_target_pairs={{1,0},{0,1},{3,2},{2,3},{5,4},{4,5},{7,6},{6,7},{9,8},{8,9},{11,10... | collective-permute-start | bytes 786440 | tf_op jit(solution)/shard_map/ppermute | solution.py:258
  8.3 1.4 %copy-start = (bf16[2048,384]{1,0:T(8,128)(2,1)S(1)}, bf16[2048,384]{1,0:T(8,128)(2,1)}, u32[]{:S(2)}) copy-start(bf16[2048,384]{1,0:T(8,128)(2,1)} %w_out_ref.3) | copy-start | bytes 4718596
  9.7 1.4 %copy-start.1 = (bf16[2048,384]{1,0:T(8,128)(2,1)S(1)}, bf16[2048,384]{1,0:T(8,128)(2,1)}, u32[]{:S(2)}) copy-start(bf16[2048,384]{1,0:T(8,128)(2,1)} %w_in_ref.3) | copy-start | bytes 4718596
  11.1 0.9 %copy-start.4 = (bf16[128,384]{1,0:T(8,128)(2,1)S(1)}, bf16[128,384]{1,0:T(8,128)(2,1)}, u32[]{:S(2)}) copy-start(bf16[128,384]{1,0:T(8,128)(2,1)} %pre_ref.4) | copy-start | bytes 294916
  12.0 1.4 %copy-start.3 = (f32[32,2048]{1,0:T(8,128)S(1)}, f32[32,2048]{1,0:T(8,128)}, u32[]{:S(2)}) copy-start(f32[32,2048]{1,0:T(8,128)} %lower_ref.1) | copy-start | bytes 786436
  13.0 8.5 %collective-permute-start.2 = (bf16[32,2048]{1,0:T(8,128)(2,1)S(1)}, bf16[32,2048]{1,0:T(8,128)(2,1)S(1)}, u32[]{:S(2)}, u32[]{:S(2)}) collective-permute-start(bf16[32,2048]{1,0:T(8,128)(2,1)S(1)} %collective-permute-done.1.refs_1_.refs_2_), channel_id=1, source_target_pairs={{1,0},{0,1},{3,2},{2,3},{5,4},{4,5},{7,6},{6,7},{9,8},{8,9},{11,10... | collective-permute-start | bytes 393224 | tf_op jit(solution)/shard_map/ppermute | solution.py:258
  13.5 10.5 %collective-permute-start.6 = (bf16[32,2048]{1,0:T(8,128)(2,1)S(1)}, bf16[32,2048]{1,0:T(8,128)(2,1)S(1)}, u32[]{:S(2)}, u32[]{:S(2)}) collective-permute-start(bf16[32,2048]{1,0:T(8,128)(2,1)S(1)} %convert_element_type.7.refs_0_), channel_id=1, source_target_pairs={{2,0},{3,1},{0,2},{1,3},{6,4},{7,5},{4,6},{5,7},{10,8},{11,9},{8,1... | collective-permute-start | bytes 393224 | tf_op jit(solution)/shard_map/ppermute | solution.py:258
  22.4 6.2 %collective-permute-start.3 = (bf16[32,2048]{1,0:T(8,128)(2,1)S(1)}, bf16[32,2048]{1,0:T(8,128)(2,1)S(1)}, u32[]{:S(2)}, u32[]{:S(2)}) collective-permute-start(bf16[32,2048]{1,0:T(8,128)(2,1)S(1)} %get-tuple-element.19), channel_id=1, source_target_pairs={{1,0},{0,1},{3,2},{2,3},{5,4},{4,5},{7,6},{6,7},{9,8},{8,9},{11,10... | collective-permute-start | bytes 393224 | tf_op jit(solution)/shard_map/ppermute | solution.py:258
  24.0 8.1 %collective-permute-start.7 = (bf16[32,2048]{1,0:T(8,128)(2,1)S(1)}, bf16[32,2048]{1,0:T(8,128)(2,1)S(1)}, u32[]{:S(2)}, u32[]{:S(2)}) collective-permute-start(bf16[32,2048]{1,0:T(8,128)(2,1)S(1)} %collective-permute-done.6.refs_2_), channel_id=1, source_target_pairs={{1,0},{0,1},{3,2},{2,3},{5,4},{4,5},{7,6},{6,7},{9,8},{8,9},{11,10... | collective-permute-start | bytes 393224 | tf_op jit(solution)/shard_map/ppermute | solution.py:258
  28.6 7.1 %collective-permute-start.4 = (bf16[32,2048]{1,0:T(8,128)(2,1)S(1)}, bf16[32,2048]{1,0:T(8,128)(2,1)S(1)}, u32[]{:S(2)}, u32[]{:S(2)}) collective-permute-start(bf16[32,2048]{1,0:T(8,128)(2,1)S(1)} %add.3), channel_id=1, source_target_pairs={{0,2},{1,3},{2,0},{3,1},{4,6},{5,7},{6,4},{7,5},{8,10},{9,11},{10,... | collective-permute-start | bytes 393224 | tf_op jit(solution)/shard_map/ppermute | solution.py:262
  29.0 6.8 %collective-permute-start.5 = (bf16[32,2048]{1,0:T(8,128)(2,1)S(1)}, bf16[32,2048]{1,0:T(8,128)(2,1)S(1)}, u32[]{:S(2)}, u32[]{:S(2)}) collective-permute-start(bf16[32,2048]{1,0:T(8,128)(2,1)S(1)} %get-tuple-element.22), channel_id=1, source_target_pairs={{1,0},{0,1},{3,2},{2,3},{5,4},{4,5},{7,6},{6,7},{9,8},{8,9},{11,10... | collective-permute-start | bytes 393224 | tf_op jit(solution)/shard_map/ppermute | solution.py:258

commit v4 on v1

--- a/solution.py
+++ b/solution.py
@@ -29,12 +29,14 @@
     return 2 if n % 2 == 0 else 1
 
 
+def crosses(slot, n):
+    return team_of(n) == 2 and (slot % 2 == 1) == (slot < 2)
+
+
 def owner(me, slot, n):
     team = team_of(n)
     ahead = lax.rem(me + slot // team * team, n)
-    if slot % team == 0:
-        return ahead
-    return ahead + 1 - 2 * lax.rem(ahead, 2)
+    return ahead + 1 - 2 * lax.rem(ahead, 2) if crosses(slot, n) else ahead
 
 
 def pre_block(ref, me, slot, n, rows):
@@ -218,7 +220,7 @@
 
 def owner_of(me, slot, n):
     ahead = (me + slot // team_of(n) * team_of(n)) % n
-    return ahead ^ (slot % team_of(n))
+    return ahead ^ int(crosses(slot, n))
 
 
 def from_slot(n, block, slot):

time: 36.8 us -> 36.5 us (level)
  starting transfers between devices: 14 us -> 10.9 us
  waiting for transfers between devices: 10.6 us -> 13.4 us
    ppermute x7, starting transfers between devices: 13.7 us -> 9.93 us  [from_slot(): lax.ppermute(block, AXIS, [(owner_of(i, slot, n), i) for i in range(n)])]
    ppermute x7, waiting for transfers between devices: 8.36 us -> 11.2 us  [from_slot(): lax.ppermute(block, AXIS, [(owner_of(i, slot, n), i) for i in range(n)])]
    ppermute x1, starting transfers between devices: 0.33 us -> 0.93 us  [to_slot(): lax.ppermute(block, AXIS, [(i, owner_of(i, slot, n)) for i in range(n)])]
where the time goes in v4:
time: 36.5 us; the launch traced here: 36.3 us
  waiting for transfers between devices  13.4 us (37%)
  starting transfers between devices  10.9 us (30%)
  Pallas kernels  4.83 us (13%)
  local copies, waits for them, and re-layouts  4.66 us (13%)
  other arithmetic  1.75 us (5%)
  between operations  0.71 us (2%)
    ppermute x7, waiting for transfers between devices, from_slot(): lax.ppermute(block, AXIS, [(owner_of(i, slot, n), i) for i in range(n)])  11.2 us
    ppermute x7, starting transfers between devices, from_slot(): lax.ppermute(block, AXIS, [(owner_of(i, slot, n), i) for i in range(n)])  9.93 us
    unnamed x14, local copies, waits for them, and re-layouts  4.66 us
    ppermute x1, waiting for transfers between devices, to_slot(): lax.ppermute(block, AXIS, [(i, owner_of(i, slot, n)) for i in range(n)])  2.21 us
    pallas_call x1, Pallas kernels, out_weight_grad(): pl.pallas_call(functools.partial(out_kernel, n, starts), out_shape=jax.Sh...  1.46 us
    pallas_call x1, Pallas kernels, in_weight_grad(): pl.pallas_call(functools.partial(in_kernel, n, starts, len(hids)), out_sh...  1.46 us
    convert_element_type x1, other arithmetic, on_device(): grad_bf = out_grad.astype(jnp.bfloat16)  0.97 us
    pallas_call x1, Pallas kernels, partials(): pl.pallas_call(functools.partial(partial_kernel, n, starts), out_shape=[j...  0.96 us
  transfers between devices with their start and end apart: 8, of which 6 were waited for; matrix products, arithmetic and copies ran while one was open for 0% of the time, Pallas kernels for 13%

profile of v4, /device:TPU:0, one launch (start us, length us, event | category | flops | bytes accessed | tf_op | source)
XLA Modules:
  0.0 36.3 jit_solution(8017165104883007830)
XLA Ops:
  0.6 1.0 %convert_element_type.12.grad_ref.upper_ref.refs_0_ = bf16[32,2048]{1,0:T(8,128)(2,1)S(1)} convert(f32[32,2048]{1,0:T(8,128)} %param.6) | non-fusion elementwise | flops 65536 | bytes 393216 | tf_op jit(solution)/shard_map/convert_element_type | solution.py:243
  1.6 5.1 %collective-permute-start.1 = (bf16[32,2048]{1,0:T(8,128)(2,1)S(1)}, bf16[32,2048]{1,0:T(8,128)(2,1)S(1)}, u32[]{:S(2)}, u32[]{:S(2)}) collective-permute-start(bf16[32,2048]{1,0:T(8,128)(2,1)S(1)} %convert_element_type.12.grad_ref.upper_ref.refs_0_), channel_id=1, source_target_pairs={{3,0},{2,1},{1,2},{0,3},{7,4},{6,5},{5,6},{4,7},{11,8},{10,9},{9,1... | collective-permute-start | bytes 393224 | tf_op jit(solution)/shard_map/ppermute | solution.py:227
  6.7 0.0 copy-start.4
  6.7 0.9 %copy-done.4 = f32[32,2048]{1,0:T(8,128)S(1)} copy-done((f32[32,2048]{1,0:T(8,128)S(1)}, f32[32,2048]{1,0:T(8,128)}, u32[]{:S(2)}) %copy-start.4) | copy-done | bytes 262168
  7.7 0.0 copy-start.5
  7.7 0.1 collective-permute-start
  7.8 0.0 copy-start
  7.8 1.4 %copy-done = bf16[2048,384]{1,0:T(8,128)(2,1)S(1)} copy-done((bf16[2048,384]{1,0:T(8,128)(2,1)S(1)}, bf16[2048,384]{1,0:T(8,128)(2,1)}, u32[]{:S(2)}) %copy-start) | copy-done | bytes 1572888
  9.2 0.0 copy-start.2
  9.2 1.4 %copy-done.2 = bf16[2048,384]{1,0:T(8,128)(2,1)S(1)} copy-done((bf16[2048,384]{1,0:T(8,128)(2,1)S(1)}, bf16[2048,384]{1,0:T(8,128)(2,1)}, u32[]{:S(2)}) %copy-start.2) | copy-done | bytes 1572888
  10.6 0.0 copy-start.6
  10.6 0.9 %copy-done.6 = bf16[128,384]{1,0:T(8,128)(2,1)S(1)} copy-done((bf16[128,384]{1,0:T(8,128)(2,1)S(1)}, bf16[128,384]{1,0:T(8,128)(2,1)}, u32[]{:S(2)}) %copy-start.6) | copy-done | bytes 98328
  11.5 0.0 copy-start.1
  11.5 0.0 copy-start.3
  11.5 0.9 %own_block.1 = (bf16[32,384]{1,0:T(8,128)(2,1)S(1)}, f32[32,2048]{1,0:T(8,128)S(1)}) custom-call(s32[1]{0:T(128)} %bitcast.me_ref, bf16[128,384]{1,0:T(8,128)(2,1)S(1)} %copy-done.6, bf16[2048,384]{1,0:T(8,128)(2,1)S(1)} %copy-done, bf16[2048,384]{1,0:T(8,128)(2,1)S(1)} %copy-done.2, bf16[32,2048]{1,0:T(8,128)(2,1)S(1)} %convert_element_type.12.grad_ref.upper_ref.refs_0_), custom_call_target="tpu_custom_call" | custom-call | flops 100663296 | bytes 3538944 | tf_op jit(solution)/shard_map/own_block/pallas_call | solution.py:99
  12.4 0.0 collective-permute-done.1.refs_1_.refs_2_
  12.4 2.0 %collective-permute-start.2 = (bf16[32,2048]{1,0:T(8,128)(2,1)S(1)}, bf16[32,2048]{1,0:T(8,128)(2,1)S(1)}, u32[]{:S(2)}, u32[]{:S(2)}) collective-permute-start(bf16[32,2048]{1,0:T(8,128)(2,1)S(1)} %collective-permute-done.1.refs_1_.refs_2_), channel_id=1, source_target_pairs={{1,0},{0,1},{3,2},{2,3},{5,4},{4,5},{7,6},{6,7},{9,8},{8,9},{11,10... | collective-permute-start | bytes 393224 | tf_op jit(solution)/shard_map/ppermute | solution.py:227
  14.5 0.0 copy-done.5
  14.5 0.6 %collective-permute-start.6 = (bf16[32,2048]{1,0:T(8,128)(2,1)S(1)}, bf16[32,2048]{1,0:T(8,128)(2,1)S(1)}, u32[]{:S(2)}, u32[]{:S(2)}) collective-permute-start(bf16[32,2048]{1,0:T(8,128)(2,1)S(1)} %convert_element_type.15.refs_0_), channel_id=1, source_target_pairs={{3,0},{2,1},{1,2},{0,3},{7,4},{6,5},{5,6},{4,7},{11,8},{10,9},{9,1... | collective-permute-start | bytes 393224 | tf_op jit(solution)/shard_map/ppermute | solution.py:227
  15.0 2.0 %collective-permute-done.refs_0_.refs_1_ = bf16[64,2048]{1,0:T(8,128)(2,1)S(1)} collective-permute-done((bf16[64,2048]{1,0:T(8,128)(2,1)S(1)}, bf16[64,2048]{1,0:T(8,128)(2,1)S(1)}, u32[]{:S(2)}, u32[]{:S(2)}) %collective-permute-start) | collective-permute-done | bytes 262176 | tf_op jit(solution)/shard_map/ppermute | solution.py:227
  17.0 4.7 %collective-permute-done.2.refs_2_.refs_3_ = bf16[32,2048]{1,0:T(8,128)(2,1)S(1)} collective-permute-done((bf16[32,2048]{1,0:T(8,128)(2,1)S(1)}, bf16[32,2048]{1,0:T(8,128)(2,1)S(1)}, u32[]{:S(2)}, u32[]{:S(2)}) %collective-permute-start.2) | collective-permute-done | bytes 131104 | tf_op jit(solution)/shard_map/ppermute | solution.py:227
  21.7 0.0 copy-done.1
  21.7 0.0 copy-done.3
  21.7 1.0 %partials.1 = (bf16[96,384]{1,0:T(8,128)(2,1)S(1)}, bf16[32,2048]{1,0:T(8,128)(2,1)S(1)}, bf16[32,2048]{1,0:T(8,128)(2,1)S(1)}, bf16[32,2048]{1,0:T(8,128)(2,1)S(1)}) custom-call(s32[1]{0:T(128)} %bitcast.me_ref, bf16[128,384]{1,0:T(8,128)(2,1)S(1)} %copy-done.6, bf16[2048,384]{1,0:T(8,128)(2,1)S(1)} %copy-done.1, bf16[2048,384]{1,0:T(8,128)(2,1)S(1)} %copy-done.3, ...), custom_call_target="tpu_custom_call" | custom-call | flops 301989888 | bytes 4079616 | tf_op jit(solution)/shard_map/partials/pallas_call | solution.py:132
  22.7 0.1 collective-permute-start.3
  22.8 1.5 %out_weight_grad.1 = bf16[2048,384]{1,0:T(8,128)(2,1)} custom-call(s32[1]{0:T(128)} %bitcast.me_ref, bf16[128,384]{1,0:T(8,128)(2,1)S(1)} %copy-done.6, bf16[32,2048]{1,0:T(8,128)(2,1)S(1)} %convert_element_type.12.grad_ref.upper_ref.refs_0_, bf16[64,2048]{1,0:T(8,128)(2,1)S(1)} %collective-permute-done.refs_0_.refs_1_, ...), custom_call_target="tpu_custom_call" | custom-call | flops 201326592 | bytes 2195456 | tf_op jit(solution)/shard_map/out_weight_grad/pallas_call | solution.py:194
  24.2 0.0 collective-permute-done.6.refs_2_
  24.3 2.1 %collective-permute-start.7 = (bf16[32,2048]{1,0:T(8,128)(2,1)S(1)}, bf16[32,2048]{1,0:T(8,128)(2,1)S(1)}, u32[]{:S(2)}, u32[]{:S(2)}) collective-permute-start(bf16[32,2048]{1,0:T(8,128)(2,1)S(1)} %collective-permute-done.6.refs_2_), channel_id=1, source_target_pairs={{1,0},{0,1},{3,2},{2,3},{5,4},{4,5},{7,6},{6,7},{9,8},{8,9},{11,10... | collective-permute-start | bytes 393224 | tf_op jit(solution)/shard_map/ppermute | solution.py:227
  26.3 1.8 %collective-permute-done.3 = bf16[32,2048]{1,0:T(8,128)(2,1)S(1)} collective-permute-done((bf16[32,2048]{1,0:T(8,128)(2,1)S(1)}, bf16[32,2048]{1,0:T(8,128)(2,1)S(1)}, u32[]{:S(2)}, u32[]{:S(2)}) %collective-permute-start.3) | collective-permute-done | bytes 131104 | tf_op jit(solution)/shard_map/ppermute | solution.py:227
  28.2 0.9 %collective-permute-start.4 = (bf16[32,2048]{1,0:T(8,128)(2,1)S(1)}, bf16[32,2048]{1,0:T(8,128)(2,1)S(1)}, u32[]{:S(2)}, u32[]{:S(2)}) collective-permute-start(bf16[32,2048]{1,0:T(8,128)(2,1)S(1)} %add.9), channel_id=1, source_target_pairs={{0,3},{1,2},{2,1},{3,0},{4,7},{5,6},{6,5},{7,4},{8,11},{9,10},{10,... | collective-permute-start | bytes 393224 | tf_op jit(solution)/shard_map/ppermute | solution.py:231
  29.1 0.0 collective-permute-start.5
  29.2 2.3 %collective-permute-done.7.refs_3_ = bf16[32,2048]{1,0:T(8,128)(2,1)S(1)} collective-permute-done((bf16[32,2048]{1,0:T(8,128)(2,1)S(1)}, bf16[32,2048]{1,0:T(8,128)(2,1)S(1)}, u32[]{:S(2)}, u32[]{:S(2)}) %collective-permute-start.7) | collective-permute-done | bytes 131104 | tf_op jit(solution)/shard_map/ppermute | solution.py:227
  31.5 1.5 %in_weight_grad.1 = bf16[2048,384]{1,0:T(8,128)(2,1)} custom-call(bf16[32,2048]{1,0:T(8,128)(2,1)S(1)} %convert_element_type.15.refs_0_, bf16[64,2048]{1,0:T(8,128)(2,1)S(1)} %collective-permute-done.refs_0_.refs_1_, bf16[32,2048]{1,0:T(8,128)(2,1)S(1)} %collective-permute-done.6.refs_2_, bf16[32,2048]{1,0:T(8,128)(2,1)S(1)} %collective-permute-done.7.refs_3_, ...), custom_call_target="tpu_custom_call" | custom-call | flops 201326592 | bytes 2195456 | tf_op jit(solution)/shard_map/in_weight_grad/pallas_call | solution.py:209
  32.9 2.2 %collective-permute-done.4 = bf16[32,2048]{1,0:T(8,128)(2,1)S(1)} collective-permute-done((bf16[32,2048]{1,0:T(8,128)(2,1)S(1)}, bf16[32,2048]{1,0:T(8,128)(2,1)S(1)}, u32[]{:S(2)}, u32[]{:S(2)}) %collective-permute-start.4) | collective-permute-done | bytes 131104 | tf_op jit(solution)/shard_map/ppermute | solution.py:231
  35.2 0.4 %collective-permute-done.5 = bf16[32,2048]{1,0:T(8,128)(2,1)S(1)} collective-permute-done((bf16[32,2048]{1,0:T(8,128)(2,1)S(1)}, bf16[32,2048]{1,0:T(8,128)(2,1)S(1)}, u32[]{:S(2)}, u32[]{:S(2)}) %collective-permute-start.5) | collective-permute-done | bytes 131104 | tf_op jit(solution)/shard_map/ppermute | solution.py:227
  35.5 0.7 %convert_add_fusion = f32[32,2048]{1,0:T(8,128)} fusion(bf16[32,2048]{1,0:T(8,128)(2,1)S(1)} %collective-permute-done.5, f32[32,2048]{1,0:T(8,128)S(1)} %get-tuple-element.15, bf16[32,2048]{1,0:T(8,128)(2,1)S(1)} %collective-permute-done.4), kind=kLoop, calls=%fused_computation | loop fusion | flops 262144 | bytes 786432 | tf_op jit(solution)/shard_map/add | solution.py:279
  (3 shorter events, 0.1 us)
Async XLA Ops:
  1.6 10.8 %collective-permute-start.1 = (bf16[32,2048]{1,0:T(8,128)(2,1)S(1)}, bf16[32,2048]{1,0:T(8,128)(2,1)S(1)}, u32[]{:S(2)}, u32[]{:S(2)}) collective-permute-start(bf16[32,2048]{1,0:T(8,128)(2,1)S(1)} %convert_element_type.12.grad_ref.upper_ref.refs_0_), channel_id=1, source_target_pairs={{3,0},{2,1},{1,2},{0,3},{7,4},{6,5},{5,6},{4,7},{11,8},{10,9},{9,1... | collective-permute-start | bytes 393224 | tf_op jit(solution)/shard_map/ppermute | solution.py:227
  6.7 0.9 %copy-start.4 = (f32[32,2048]{1,0:T(8,128)S(1)}, f32[32,2048]{1,0:T(8,128)}, u32[]{:S(2)}) copy-start(f32[32,2048]{1,0:T(8,128)} %lower_ref.1) | copy-start | bytes 786436
  7.7 6.8 %copy-start.5 = (f32[32,2048]{1,0:T(8,128)S(1)}, f32[32,2048]{1,0:T(8,128)}, u32[]{:S(2)}) copy-start(f32[32,2048]{1,0:T(8,128)} %lower_ref.1) | copy-start | bytes 786436
  7.7 9.3 %collective-permute-start = (bf16[64,2048]{1,0:T(8,128)(2,1)S(1)}, bf16[64,2048]{1,0:T(8,128)(2,1)S(1)}, u32[]{:S(2)}, u32[]{:S(2)}) collective-permute-start(bf16[64,2048]{1,0:T(8,128)(2,1)S(1)} %pair.1), channel_id=1, source_target_pairs={{1,0},{0,1},{3,2},{2,3},{5,4},{4,5},{7,6},{6,7},{9,8},{8,9},{11,10... | collective-permute-start | bytes 786440 | tf_op jit(solution)/shard_map/ppermute | solution.py:227
  7.8 1.4 %copy-start = (bf16[2048,384]{1,0:T(8,128)(2,1)S(1)}, bf16[2048,384]{1,0:T(8,128)(2,1)}, u32[]{:S(2)}) copy-start(bf16[2048,384]{1,0:T(8,128)(2,1)} %w_out_ref.3) | copy-start | bytes 4718596
  9.2 1.4 %copy-start.2 = (bf16[2048,384]{1,0:T(8,128)(2,1)S(1)}, bf16[2048,384]{1,0:T(8,128)(2,1)}, u32[]{:S(2)}) copy-start(bf16[2048,384]{1,0:T(8,128)(2,1)} %w_in_ref.3) | copy-start | bytes 4718596
  10.6 0.9 %copy-start.6 = (bf16[128,384]{1,0:T(8,128)(2,1)S(1)}, bf16[128,384]{1,0:T(8,128)(2,1)}, u32[]{:S(2)}) copy-start(bf16[128,384]{1,0:T(8,128)(2,1)} %pre_ref.4) | copy-start | bytes 294916
  11.5 10.2 %copy-start.1 = (bf16[2048,384]{1,0:T(8,128)(2,1)S(1)}, bf16[2048,384]{1,0:T(8,128)(2,1)}, u32[]{:S(2)}) copy-start(bf16[2048,384]{1,0:T(8,128)(2,1)} %w_out_ref.3) | copy-start | bytes 4718596
  11.5 10.2 %copy-start.3 = (bf16[2048,384]{1,0:T(8,128)(2,1)S(1)}, bf16[2048,384]{1,0:T(8,128)(2,1)}, u32[]{:S(2)}) copy-start(bf16[2048,384]{1,0:T(8,128)(2,1)} %w_in_ref.3) | copy-start | bytes 4718596
  12.4 9.3 %collective-permute-start.2 = (bf16[32,2048]{1,0:T(8,128)(2,1)S(1)}, bf16[32,2048]{1,0:T(8,128)(2,1)S(1)}, u32[]{:S(2)}, u32[]{:S(2)}) collective-permute-start(bf16[32,2048]{1,0:T(8,128)(2,1)S(1)} %collective-permute-done.1.refs_1_.refs_2_), channel_id=1, source_target_pairs={{1,0},{0,1},{3,2},{2,3},{5,4},{4,5},{7,6},{6,7},{9,8},{8,9},{11,10... | collective-permute-start | bytes 393224 | tf_op jit(solution)/shard_map/ppermute | solution.py:227
  14.5 9.8 %collective-permute-start.6 = (bf16[32,2048]{1,0:T(8,128)(2,1)S(1)}, bf16[32,2048]{1,0:T(8,128)(2,1)S(1)}, u32[]{:S(2)}, u32[]{:S(2)}) collective-permute-start(bf16[32,2048]{1,0:T(8,128)(2,1)S(1)} %convert_element_type.15.refs_0_), channel_id=1, source_target_pairs={{3,0},{2,1},{1,2},{0,3},{7,4},{6,5},{5,6},{4,7},{11,8},{10,9},{9,1... | collective-permute-start | bytes 393224 | tf_op jit(solution)/shard_map/ppermute | solution.py:227
  22.7 5.5 %collective-permute-start.3 = (bf16[32,2048]{1,0:T(8,128)(2,1)S(1)}, bf16[32,2048]{1,0:T(8,128)(2,1)S(1)}, u32[]{:S(2)}, u32[]{:S(2)}) collective-permute-start(bf16[32,2048]{1,0:T(8,128)(2,1)S(1)} %get-tuple-element.19), channel_id=1, source_target_pairs={{1,0},{0,1},{3,2},{2,3},{5,4},{4,5},{7,6},{6,7},{9,8},{8,9},{11,10... | collective-permute-start | bytes 393224 | tf_op jit(solution)/shard_map/ppermute | solution.py:227
  24.3 7.2 %collective-permute-start.7 = (bf16[32,2048]{1,0:T(8,128)(2,1)S(1)}, bf16[32,2048]{1,0:T(8,128)(2,1)S(1)}, u32[]{:S(2)}, u32[]{:S(2)}) collective-permute-start(bf16[32,2048]{1,0:T(8,128)(2,1)S(1)} %collective-permute-done.6.refs_2_), channel_id=1, source_target_pairs={{1,0},{0,1},{3,2},{2,3},{5,4},{4,5},{7,6},{6,7},{9,8},{8,9},{11,10... | collective-permute-start | bytes 393224 | tf_op jit(solution)/shard_map/ppermute | solution.py:227
  28.2 6.9 %collective-permute-start.4 = (bf16[32,2048]{1,0:T(8,128)(2,1)S(1)}, bf16[32,2048]{1,0:T(8,128)(2,1)S(1)}, u32[]{:S(2)}, u32[]{:S(2)}) collective-permute-start(bf16[32,2048]{1,0:T(8,128)(2,1)S(1)} %add.9), channel_id=1, source_target_pairs={{0,3},{1,2},{2,1},{3,0},{4,7},{5,6},{6,5},{7,4},{8,11},{9,10},{10,... | collective-permute-start | bytes 393224 | tf_op jit(solution)/shard_map/ppermute | solution.py:231
  29.1 6.4 %collective-permute-start.5 = (bf16[32,2048]{1,0:T(8,128)(2,1)S(1)}, bf16[32,2048]{1,0:T(8,128)(2,1)S(1)}, u32[]{:S(2)}, u32[]{:S(2)}) collective-permute-start(bf16[32,2048]{1,0:T(8,128)(2,1)S(1)} %get-tuple-element.22), channel_id=1, source_target_pairs={{1,0},{0,1},{3,2},{2,3},{5,4},{4,5},{7,6},{6,7},{9,8},{8,9},{11,10... | collective-permute-start | bytes 393224 | tf_op jit(solution)/shard_map/ppermute | solution.py:227

commit v5 on v4

--- a/solution.py
+++ b/solution.py
@@ -45,25 +45,6 @@
 
 def stack(refs, starts, rows, columns=slice(None)):
     return jnp.concatenate([ref[s : s + rows, columns] for ref, s in zip(refs, starts)], axis=0)
-
-
-def pair_kernel(upper_ref, lower_ref, both_ref):
-    rows = upper_ref.shape[0]
-    both_ref[:rows, :] = upper_ref[...]
-    both_ref[rows:, :] = lower_ref[...].astype(both_ref.dtype)
-
-
-def pair(upper, lower):
-    rows, width = upper.shape
-    return pl.pallas_call(
-        pair_kernel,
-        out_shape=jax.ShapeDtypeStruct((2 * rows, width), upper.dtype),
-        in_specs=[VMEM] * 2,
-        out_specs=VMEM,
-        cost_estimate=cost(0, 10 * rows * width),
-        compiler_params=PARAMS,
-        name="pair",
-    )(upper, lower)
 
 
 def share(pre, grads, w_out_ref, w_in_ref, emit):
@@ -238,15 +219,12 @@
 def on_device(inputs, out_grad, pre_saved, w_in, w_out_t, *, n):
     team = team_of(n)
     far = range(team, n, team)
-    rows = inputs.shape[0]
     me = lax.axis_index(AXIS).astype(jnp.int32).reshape(1)
     grad_bf = out_grad.astype(jnp.bfloat16)
     far_grads = [from_slot(n, grad_bf, k) for k in far]
-    both = pair(grad_bf, inputs)
     grads, ins = {0: (grad_bf, 0)}, {}
     if team == 2:
-        near = from_slot(n, both, 1)
-        grads[1], ins[1] = (near, 0), (near, rows)
+        grads[1] = (from_slot(n, grad_bf, 1), 0)
     own_hid, input_grad = own_block(n, me, pre_saved, w_out_t, w_in, grad_bf)
     hids = [own_hid]
     far_grads = later(far_grads, own_hid)
@@ -257,25 +235,31 @@
     inputs_bf = later(inputs, far_grads).astype(jnp.bfloat16)
     ins[0] = (inputs_bf, 0)
     far_ins = [from_slot(n, inputs_bf, k) for k in far]
+    near = from_slot(n, inputs_bf, 1) if team == 2 else inputs_bf
     arrived, pre = [], pre_saved
     if n > 1:
         hid, *parts = partials(n, me, pre_saved, w_out_t, w_in, [grads[k] for k in range(1, n)])
-        pre = later(pre, parts)
+        near, pre = lax.optimization_barrier((near, later(pre, parts, far_ins)))
+        if team == 2:
+            ins[1] = (near, 0)
         parts = [None] + parts
         hids.append(hid)
+        grad_w_out_t = out_weight_grad(n, me, [grads[k] for k in range(n)], pre)
         sums = [parts[k] + from_slot(n, parts[k + 1], 1) if team == 2 else parts[k] for k in far]
-        sums, parts = lax.optimization_barrier((sums, parts))
+        sums, parts, far_ins, grad_w_out_t = lax.optimization_barrier(
+            (sums, parts, far_ins, grad_w_out_t)
+        )
         arrived = [to_slot(n, block, k) for k, block in zip(far, sums)]
         if team == 2:
             arrived.append(from_slot(n, parts[1], 1))
-    grad_w_out_t = out_weight_grad(n, me, [grads[k] for k in range(n)], pre)
-    far_ins = later(far_ins, grad_w_out_t)
+    else:
+        grad_w_out_t = out_weight_grad(n, me, [grads[0]], pre)
     for k, got in zip(far, far_ins):
         ins[k] = (got, 0)
         if team == 2:
             ins[k + 1] = (from_slot(n, got, 1), 0)
     grad_w_in = in_weight_grad(n, [ins[k] for k in range(n)], hids)
-    for block in arrived:
+    for block in later(arrived, grad_w_in):
         input_grad = input_grad + block.astype(jnp.float32)
     return (input_grad, grad_w_in, grad_w_out_t)
 

time: 36.5 us -> 36 us (0.986)
  starting transfers between devices: 10.9 us -> 16.8 us
  waiting for transfers between devices: 13.4 us -> 8.06 us
  local copies, waits for them, and re-layouts: 4.66 us -> 3.71 us
    ppermute x7 -> x8, starting transfers between devices: 9.93 us -> 14.7 us  [from_slot(): lax.ppermute(block, AXIS, [(owner_of(i, slot, n), i) for i in range(n)])]
    ppermute x7 -> x8, waiting for transfers between devices: 11.2 us -> 6.77 us  [from_slot(): lax.ppermute(block, AXIS, [(owner_of(i, slot, n), i) for i in range(n)])]
    ppermute x1, starting transfers between devices: 0.93 us -> 2.06 us  [to_slot(): lax.ppermute(block, AXIS, [(i, owner_of(i, slot, n)) for i in range(n)])]
    unnamed x14 -> x8, local copies, waits for them, and re-layouts: 4.66 us -> 3.71 us
    ppermute x1, waiting for transfers between devices: 2.21 us -> 1.28 us  [to_slot(): lax.ppermute(block, AXIS, [(i, owner_of(i, slot, n)) for i in range(n)])]
  transfers between devices with their start and end apart: 8 -> 9, of which waited for: 6 -> 5; matrix products, arithmetic and copies ran while one was open for 0% -> 0% of each run, Pallas kernels for 13% -> 13%
where the time goes in v5:
time: 36 us; the launch traced here: 35.8 us
  starting transfers between devices  16.8 us (47%)
  waiting for transfers between devices  8.06 us (22%)
  Pallas kernels  4.79 us (13%)
  local copies, waits for them, and re-layouts  3.71 us (10%)
  other arithmetic  1.76 us (5%)
  between operations  0.68 us (2%)
    ppermute x8, starting transfers between devices, from_slot(): lax.ppermute(block, AXIS, [(owner_of(i, slot, n), i) for i in range(n)])  14.7 us
    ppermute x8, waiting for transfers between devices, from_slot(): lax.ppermute(block, AXIS, [(owner_of(i, slot, n), i) for i in range(n)])  6.77 us
    unnamed x8, local copies, waits for them, and re-layouts  3.71 us
    ppermute x1, starting transfers between devices, to_slot(): lax.ppermute(block, AXIS, [(i, owner_of(i, slot, n)) for i in range(n)])  2.06 us
    pallas_call x1, Pallas kernels, out_weight_grad(): pl.pallas_call(functools.partial(out_kernel, n, starts), out_shape=jax.Sh...  1.46 us
    pallas_call x1, Pallas kernels, in_weight_grad(): pl.pallas_call(functools.partial(in_kernel, n, starts, len(hids)), out_sh...  1.46 us
    ppermute x1, waiting for transfers between devices, to_slot(): lax.ppermute(block, AXIS, [(i, owner_of(i, slot, n)) for i in range(n)])  1.28 us
    convert_element_type x1, other arithmetic, on_device(): grad_bf = out_grad.astype(jnp.bfloat16)  0.97 us
  transfers between devices with their start and end apart: 9, of which 5 were waited for; matrix products, arithmetic and copies ran while one was open for 0% of the time, Pallas kernels for 13%

profile of v5, /device:TPU:0, one launch (start us, length us, event | category | flops | bytes accessed | tf_op | source)
XLA Modules:
  0.0 35.8 jit_solution(13640399203883689054)
XLA Ops:
  0.6 1.0 %convert_element_type.12.grad_ref.refs_0_ = bf16[32,2048]{1,0:T(8,128)(2,1)S(1)} convert(f32[32,2048]{1,0:T(8,128)} %param.6) | non-fusion elementwise | flops 65536 | bytes 393216 | tf_op jit(solution)/shard_map/convert_element_type | solution.py:223
  1.6 5.1 %collective-permute-start.1 = (bf16[32,2048]{1,0:T(8,128)(2,1)S(1)}, bf16[32,2048]{1,0:T(8,128)(2,1)S(1)}, u32[]{:S(2)}, u32[]{:S(2)}) collective-permute-start(bf16[32,2048]{1,0:T(8,128)(2,1)S(1)} %convert_element_type.12.grad_ref.refs_0_), channel_id=1, source_target_pairs={{3,0},{2,1},{1,2},{0,3},{7,4},{6,5},{5,6},{4,7},{11,8},{10,9},{9,1... | collective-permute-start | bytes 393224 | tf_op jit(solution)/shard_map/ppermute | solution.py:208
  6.7 0.0 collective-permute-start
  6.7 0.0 copy-start
  6.7 1.4 %copy-done = bf16[2048,384]{1,0:T(8,128)(2,1)S(1)} copy-done((bf16[2048,384]{1,0:T(8,128)(2,1)S(1)}, bf16[2048,384]{1,0:T(8,128)(2,1)}, u32[]{:S(2)}) %copy-start) | copy-done | bytes 1572888
  8.1 0.0 copy-start.1
  8.1 1.4 %copy-done.1 = bf16[2048,384]{1,0:T(8,128)(2,1)S(1)} copy-done((bf16[2048,384]{1,0:T(8,128)(2,1)S(1)}, bf16[2048,384]{1,0:T(8,128)(2,1)}, u32[]{:S(2)}) %copy-start.1) | copy-done | bytes 1572888
  9.5 0.0 copy-start.2
  9.5 0.9 %copy-done.2 = bf16[128,384]{1,0:T(8,128)(2,1)S(1)} copy-done((bf16[128,384]{1,0:T(8,128)(2,1)S(1)}, bf16[128,384]{1,0:T(8,128)(2,1)}, u32[]{:S(2)}) %copy-start.2) | copy-done | bytes 98328
  10.4 0.0 copy-start.3
  10.4 0.9 %own_block.1 = (bf16[32,384]{1,0:T(8,128)(2,1)S(1)}, f32[32,2048]{1,0:T(8,128)S(1)}) custom-call(s32[1]{0:T(128)} %bitcast.me_ref, bf16[128,384]{1,0:T(8,128)(2,1)S(1)} %copy-done.2, bf16[2048,384]{1,0:T(8,128)(2,1)S(1)} %copy-done, bf16[2048,384]{1,0:T(8,128)(2,1)S(1)} %copy-done.1, bf16[32,2048]{1,0:T(8,128)(2,1)S(1)} %convert_element_type.12.grad_ref.refs_0_), custom_call_target="tpu_custom_call" | custom-call | flops 100663296 | bytes 3538944 | tf_op jit(solution)/shard_map/own_block/pallas_call | solution.py:80
  11.4 0.0 collective-permute-done.1.refs_1_.refs_2_
  11.4 2.1 %collective-permute-start.2 = (bf16[32,2048]{1,0:T(8,128)(2,1)S(1)}, bf16[32,2048]{1,0:T(8,128)(2,1)S(1)}, u32[]{:S(2)}, u32[]{:S(2)}) collective-permute-start(bf16[32,2048]{1,0:T(8,128)(2,1)S(1)} %collective-permute-done.1.refs_1_.refs_2_), channel_id=1, source_target_pairs={{1,0},{0,1},{3,2},{2,3},{5,4},{4,5},{7,6},{6,7},{9,8},{8,9},{11,10... | collective-permute-start | bytes 393224 | tf_op jit(solution)/shard_map/ppermute | solution.py:208
  13.4 0.0 copy-done.3
  13.4 0.1 collective-permute-start.5
  13.5 3.5 %collective-permute-start.4 = (bf16[32,2048]{1,0:T(8,128)(2,1)S(1)}, bf16[32,2048]{1,0:T(8,128)(2,1)S(1)}, u32[]{:S(2)}, u32[]{:S(2)}) collective-permute-start(bf16[32,2048]{1,0:T(8,128)(2,1)S(1)} %convert_element_type.13.refs_0_), channel_id=1, source_target_pairs={{3,0},{2,1},{1,2},{0,3},{7,4},{6,5},{5,6},{4,7},{11,8},{10,9},{9,1... | collective-permute-start | bytes 393224 | tf_op jit(solution)/shard_map/ppermute | solution.py:208
  17.0 0.0 collective-permute-done.refs_0_.refs_1_
  17.0 1.4 %collective-permute-done.2.refs_2_.refs_3_ = bf16[32,2048]{1,0:T(8,128)(2,1)S(1)} collective-permute-done((bf16[32,2048]{1,0:T(8,128)(2,1)S(1)}, bf16[32,2048]{1,0:T(8,128)(2,1)S(1)}, u32[]{:S(2)}, u32[]{:S(2)}) %collective-permute-start.2) | collective-permute-done | bytes 131104 | tf_op jit(solution)/shard_map/ppermute | solution.py:208
  18.4 0.9 %partials.1 = (bf16[96,384]{1,0:T(8,128)(2,1)S(1)}, bf16[32,2048]{1,0:T(8,128)(2,1)S(1)}, bf16[32,2048]{1,0:T(8,128)(2,1)S(1)}, bf16[32,2048]{1,0:T(8,128)(2,1)S(1)}) custom-call(s32[1]{0:T(128)} %bitcast.me_ref, bf16[128,384]{1,0:T(8,128)(2,1)S(1)} %copy-done.2, bf16[2048,384]{1,0:T(8,128)(2,1)S(1)} %copy-done, bf16[2048,384]{1,0:T(8,128)(2,1)S(1)} %copy-done.1, ...), custom_call_target="tpu_custom_call" | custom-call | flops 301989888 | bytes 4079616 | tf_op jit(solution)/shard_map/partials/pallas_call | solution.py:113
  19.3 1.5 %collective-permute-start.3 = (bf16[32,2048]{1,0:T(8,128)(2,1)S(1)}, bf16[32,2048]{1,0:T(8,128)(2,1)S(1)}, u32[]{:S(2)}, u32[]{:S(2)}) collective-permute-start(bf16[32,2048]{1,0:T(8,128)(2,1)S(1)} %get-tuple-element.24), channel_id=1, source_target_pairs={{1,0},{0,1},{3,2},{2,3},{5,4},{4,5},{7,6},{6,7},{9,8},{8,9},{11,10... | collective-permute-start | bytes 393224 | tf_op jit(solution)/shard_map/ppermute | solution.py:208
  20.9 2.8 %collective-permute-done.4.refs_2_ = bf16[32,2048]{1,0:T(8,128)(2,1)S(1)} collective-permute-done((bf16[32,2048]{1,0:T(8,128)(2,1)S(1)}, bf16[32,2048]{1,0:T(8,128)(2,1)S(1)}, u32[]{:S(2)}, u32[]{:S(2)}) %collective-permute-start.4) | collective-permute-done | bytes 131104 | tf_op jit(solution)/shard_map/ppermute | solution.py:208
  23.7 0.0 collective-permute-done.5.refs_1_
  23.7 1.5 %out_weight_grad.1 = bf16[2048,384]{1,0:T(8,128)(2,1)} custom-call(s32[1]{0:T(128)} %bitcast.me_ref, bf16[128,384]{1,0:T(8,128)(2,1)S(1)} %copy-done.2, bf16[32,2048]{1,0:T(8,128)(2,1)S(1)} %convert_element_type.12.grad_ref.refs_0_, bf16[32,2048]{1,0:T(8,128)(2,1)S(1)} %collective-permute-done.refs_0_.refs_1_, ...), custom_call_target="tpu_custom_call" | custom-call | flops 201326592 | bytes 2195456 | tf_op jit(solution)/shard_map/out_weight_grad/pallas_call | solution.py:175
  25.2 0.0 collective-permute-done.3
  25.2 1.4 %collective-permute-start.8 = (bf16[32,2048]{1,0:T(8,128)(2,1)S(1)}, bf16[32,2048]{1,0:T(8,128)(2,1)S(1)}, u32[]{:S(2)}, u32[]{:S(2)}) collective-permute-start(bf16[32,2048]{1,0:T(8,128)(2,1)S(1)} %collective-permute-done.4.refs_2_), channel_id=1, source_target_pairs={{1,0},{0,1},{3,2},{2,3},{5,4},{4,5},{7,6},{6,7},{9,8},{8,9},{11,10... | collective-permute-start | bytes 393224 | tf_op jit(solution)/shard_map/ppermute | solution.py:208
  26.6 2.1 %collective-permute-start.6 = (bf16[32,2048]{1,0:T(8,128)(2,1)S(1)}, bf16[32,2048]{1,0:T(8,128)(2,1)S(1)}, u32[]{:S(2)}, u32[]{:S(2)}) collective-permute-start(bf16[32,2048]{1,0:T(8,128)(2,1)S(1)} %add.9), channel_id=1, source_target_pairs={{0,3},{1,2},{2,1},{3,0},{4,7},{5,6},{6,5},{7,4},{8,11},{9,10},{10,... | collective-permute-start | bytes 393224 | tf_op jit(solution)/shard_map/ppermute | solution.py:212
  28.7 1.0 %collective-permute-start.7 = (bf16[32,2048]{1,0:T(8,128)(2,1)S(1)}, bf16[32,2048]{1,0:T(8,128)(2,1)S(1)}, u32[]{:S(2)}, u32[]{:S(2)}) collective-permute-start(bf16[32,2048]{1,0:T(8,128)(2,1)S(1)} %get-tuple-element.30), channel_id=1, source_target_pairs={{1,0},{0,1},{3,2},{2,3},{5,4},{4,5},{7,6},{6,7},{9,8},{8,9},{11,10... | collective-permute-start | bytes 393224 | tf_op jit(solution)/shard_map/ppermute | solution.py:208
  29.7 2.0 %collective-permute-done.8.refs_3_ = bf16[32,2048]{1,0:T(8,128)(2,1)S(1)} collective-permute-done((bf16[32,2048]{1,0:T(8,128)(2,1)S(1)}, bf16[32,2048]{1,0:T(8,128)(2,1)S(1)}, u32[]{:S(2)}, u32[]{:S(2)}) %collective-permute-start.8) | collective-permute-done | bytes 131104 | tf_op jit(solution)/shard_map/ppermute | solution.py:208
  31.8 1.5 %in_weight_grad.1 = bf16[2048,384]{1,0:T(8,128)(2,1)} custom-call(bf16[32,2048]{1,0:T(8,128)(2,1)S(1)} %convert_element_type.13.refs_0_, bf16[32,2048]{1,0:T(8,128)(2,1)S(1)} %collective-permute-done.5.refs_1_, bf16[32,2048]{1,0:T(8,128)(2,1)S(1)} %collective-permute-done.4.refs_2_, bf16[32,2048]{1,0:T(8,128)(2,1)S(1)} %collective-permute-done.8.refs_3_, ...), custom_call_target="tpu_custom_call" | custom-call | flops 201326592 | bytes 2195456 | tf_op jit(solution)/shard_map/in_weight_grad/pallas_call | solution.py:190
  33.2 1.3 %collective-permute-done.6 = bf16[32,2048]{1,0:T(8,128)(2,1)S(1)} collective-permute-done((bf16[32,2048]{1,0:T(8,128)(2,1)S(1)}, bf16[32,2048]{1,0:T(8,128)(2,1)S(1)}, u32[]{:S(2)}, u32[]{:S(2)}) %collective-permute-start.6) | collective-permute-done | bytes 131104 | tf_op jit(solution)/shard_map/ppermute | solution.py:212
  34.5 0.5 %collective-permute-done.7 = bf16[32,2048]{1,0:T(8,128)(2,1)S(1)} collective-permute-done((bf16[32,2048]{1,0:T(8,128)(2,1)S(1)}, bf16[32,2048]{1,0:T(8,128)(2,1)S(1)}, u32[]{:S(2)}, u32[]{:S(2)}) %collective-permute-start.7) | collective-permute-done | bytes 131104 | tf_op jit(solution)/shard_map/ppermute | solution.py:208
  35.1 0.7 %convert_add_fusion = f32[32,2048]{1,0:T(8,128)} fusion(bf16[32,2048]{1,0:T(8,128)(2,1)S(1)} %collective-permute-done.7, f32[32,2048]{1,0:T(8,128)S(1)} %get-tuple-element.20, bf16[32,2048]{1,0:T(8,128)(2,1)S(1)} %collective-permute-done.6), kind=kLoop, calls=%fused_computation | loop fusion | flops 262144 | bytes 786432 | tf_op jit(solution)/shard_map/add | solution.py:263
  (2 shorter events, 0.1 us)
Async XLA Ops:
  1.6 9.8 %collective-permute-start.1 = (bf16[32,2048]{1,0:T(8,128)(2,1)S(1)}, bf16[32,2048]{1,0:T(8,128)(2,1)S(1)}, u32[]{:S(2)}, u32[]{:S(2)}) collective-permute-start(bf16[32,2048]{1,0:T(8,128)(2,1)S(1)} %convert_element_type.12.grad_ref.refs_0_), channel_id=1, source_target_pairs={{3,0},{2,1},{1,2},{0,3},{7,4},{6,5},{5,6},{4,7},{11,8},{10,9},{9,1... | collective-permute-start | bytes 393224 | tf_op jit(solution)/shard_map/ppermute | solution.py:208
  6.7 10.3 %collective-permute-start = (bf16[32,2048]{1,0:T(8,128)(2,1)S(1)}, bf16[32,2048]{1,0:T(8,128)(2,1)S(1)}, u32[]{:S(2)}, u32[]{:S(2)}) collective-permute-start(bf16[32,2048]{1,0:T(8,128)(2,1)S(1)} %convert_element_type.12.grad_ref.refs_0_), channel_id=1, source_target_pairs={{1,0},{0,1},{3,2},{2,3},{5,4},{4,5},{7,6},{6,7},{9,8},{8,9},{11,10... | collective-permute-start | bytes 393224 | tf_op jit(solution)/shard_map/ppermute | solution.py:208
  6.7 1.4 %copy-start = (bf16[2048,384]{1,0:T(8,128)(2,1)S(1)}, bf16[2048,384]{1,0:T(8,128)(2,1)}, u32[]{:S(2)}) copy-start(bf16[2048,384]{1,0:T(8,128)(2,1)} %w_out_ref.3) | copy-start | bytes 4718596
  8.1 1.4 %copy-start.1 = (bf16[2048,384]{1,0:T(8,128)(2,1)S(1)}, bf16[2048,384]{1,0:T(8,128)(2,1)}, u32[]{:S(2)}) copy-start(bf16[2048,384]{1,0:T(8,128)(2,1)} %w_in_ref.3) | copy-start | bytes 4718596
  9.5 0.9 %copy-start.2 = (bf16[128,384]{1,0:T(8,128)(2,1)S(1)}, bf16[128,384]{1,0:T(8,128)(2,1)}, u32[]{:S(2)}) copy-start(bf16[128,384]{1,0:T(8,128)(2,1)} %pre_ref.4) | copy-start | bytes 294916
  10.4 3.0 %copy-start.3 = (f32[32,2048]{1,0:T(8,128)S(1)}, f32[32,2048]{1,0:T(8,128)}, u32[]{:S(2)}) copy-start(f32[32,2048]{1,0:T(8,128)} %param.5) | copy-start | bytes 786436
  11.4 7.0 %collective-permute-start.2 = (bf16[32,2048]{1,0:T(8,128)(2,1)S(1)}, bf16[32,2048]{1,0:T(8,128)(2,1)S(1)}, u32[]{:S(2)}, u32[]{:S(2)}) collective-permute-start(bf16[32,2048]{1,0:T(8,128)(2,1)S(1)} %collective-permute-done.1.refs_1_.refs_2_), channel_id=1, source_target_pairs={{1,0},{0,1},{3,2},{2,3},{5,4},{4,5},{7,6},{6,7},{9,8},{8,9},{11,10... | collective-permute-start | bytes 393224 | tf_op jit(solution)/shard_map/ppermute | solution.py:208
  13.4 10.3 %collective-permute-start.5 = (bf16[32,2048]{1,0:T(8,128)(2,1)S(1)}, bf16[32,2048]{1,0:T(8,128)(2,1)S(1)}, u32[]{:S(2)}, u32[]{:S(2)}) collective-permute-start(bf16[32,2048]{1,0:T(8,128)(2,1)S(1)} %convert_element_type.13.refs_0_), channel_id=1, source_target_pairs={{1,0},{0,1},{3,2},{2,3},{5,4},{4,5},{7,6},{6,7},{9,8},{8,9},{11,10... | collective-permute-start | bytes 393224 | tf_op jit(solution)/shard_map/ppermute | solution.py:208
  13.5 10.2 %collective-permute-start.4 = (bf16[32,2048]{1,0:T(8,128)(2,1)S(1)}, bf16[32,2048]{1,0:T(8,128)(2,1)S(1)}, u32[]{:S(2)}, u32[]{:S(2)}) collective-permute-start(bf16[32,2048]{1,0:T(8,128)(2,1)S(1)} %convert_element_type.13.refs_0_), channel_id=1, source_target_pairs={{3,0},{2,1},{1,2},{0,3},{7,4},{6,5},{5,6},{4,7},{11,8},{10,9},{9,1... | collective-permute-start | bytes 393224 | tf_op jit(solution)/shard_map/ppermute | solution.py:208
  19.3 5.8 %collective-permute-start.3 = (bf16[32,2048]{1,0:T(8,128)(2,1)S(1)}, bf16[32,2048]{1,0:T(8,128)(2,1)S(1)}, u32[]{:S(2)}, u32[]{:S(2)}) collective-permute-start(bf16[32,2048]{1,0:T(8,128)(2,1)S(1)} %get-tuple-element.24), channel_id=1, source_target_pairs={{1,0},{0,1},{3,2},{2,3},{5,4},{4,5},{7,6},{6,7},{9,8},{8,9},{11,10... | collective-permute-start | bytes 393224 | tf_op jit(solution)/shard_map/ppermute | solution.py:208
  25.2 6.5 %collective-permute-start.8 = (bf16[32,2048]{1,0:T(8,128)(2,1)S(1)}, bf16[32,2048]{1,0:T(8,128)(2,1)S(1)}, u32[]{:S(2)}, u32[]{:S(2)}) collective-permute-start(bf16[32,2048]{1,0:T(8,128)(2,1)S(1)} %collective-permute-done.4.refs_2_), channel_id=1, source_target_pairs={{1,0},{0,1},{3,2},{2,3},{5,4},{4,5},{7,6},{6,7},{9,8},{8,9},{11,10... | collective-permute-start | bytes 393224 | tf_op jit(solution)/shard_map/ppermute | solution.py:208
  26.6 7.9 %collective-permute-start.6 = (bf16[32,2048]{1,0:T(8,128)(2,1)S(1)}, bf16[32,2048]{1,0:T(8,128)(2,1)S(1)}, u32[]{:S(2)}, u32[]{:S(2)}) collective-permute-start(bf16[32,2048]{1,0:T(8,128)(2,1)S(1)} %add.9), channel_id=1, source_target_pairs={{0,3},{1,2},{2,1},{3,0},{4,7},{5,6},{6,5},{7,4},{8,11},{9,10},{10,... | collective-permute-start | bytes 393224 | tf_op jit(solution)/shard_map/ppermute | solution.py:212
  28.7 6.4 %collective-permute-start.7 = (bf16[32,2048]{1,0:T(8,128)(2,1)S(1)}, bf16[32,2048]{1,0:T(8,128)(2,1)S(1)}, u32[]{:S(2)}, u32[]{:S(2)}) collective-permute-start(bf16[32,2048]{1,0:T(8,128)(2,1)S(1)} %get-tuple-element.30), channel_id=1, source_target_pairs={{1,0},{0,1},{3,2},{2,3},{5,4},{4,5},{7,6},{6,7},{9,8},{8,9},{11,10... | collective-permute-start | bytes 393224 | tf_op jit(solution)/shard_map/ppermute | solution.py:208
